TPU v7x, 32 devices: a whole 2x2x4 slice. The times are simulated.
32 devices in a mesh: groups: 2 (over x), row: 4 (over y, core), col: 4 (over z).
Axes of the slice: x: 2, y: 2, z: 4, core: 2. Of those that a mesh axis runs over, the one named last changes fastest.
Arguments:
- noise_field: float32 [3, 2, 4096], P(None, None, ('groups', 'row', 'col')), parts along dimension 2, may hold values from -6 to 6
- offsets: int32 [3, 4096], P(None, ('groups', 'row', 'col')), parts along dimension 1, may hold values from 0 to 7
- tile_list: int32 [8, 4, 2, 2], P(('groups', 'row'), 'col'), parts along dimension 0, may hold values from -1 to 3, as said below
- send_cells: int32 [8, 4, 16, 16], P(('groups', 'row'), 'col'), parts along dimension 0, may hold values from 0 to 131071, as said below
- bead_slot: int32 [4096], P(('groups', 'row', 'col')), parts along dimension 0, may hold values from 0 to 255, as said below
- spectral: float32 [2, 3, 2, 256, 128, 128], P(None, None, None, ('groups', 'row'), 'col'), parts along dimension 3, may hold values from -6 to 6
Outputs:
- velocity: float32 [3, 2, 4096], P(None, None, ('groups', 'row', 'col')), parts along dimension 2
There are 2 independent parts, one for each index of `groups`. A program takes and returns all parts, laid end to end along the dimension named above; each array names one. Nothing has to cross between parts.
Inputs may be any that keep to these rules, and one draw needn't show every extreme that they name: `tile_list`: for each device the first slots name distinct (row tile, column tile) pairs with row tile below 4 and column tile below 4; the remaining slots hold -1 in both entries. Some device uses all 2 slots, some device fewer. `send_cells`: entries are local cell indices of the holder's block of 128 x 32 x 32 cells, first dimension slowest. `bead_slot`: within one owner's 128 beads no value repeats, so a holder serves one owner through at most 16 slots; every owner takes all 16 slots of one holder.
All inputs are finite; a program needn't handle non-finite values.
Results may differ from a plain program's by a relative error of at most 0.0039.
Values may be sent and summed in bfloat16 or wider, within the bound.
No kernel may reach another device: no remote copies, remote signals or barrier semaphores. Data moves between devices by JAX's collectives and lax.ppermute only.
A program may use at most 128 MiB of HBM per device.

v0:
```python
import math

import jax
import jax.numpy as jnp
from jax import lax
from jax.sharding import PartitionSpec as P

TB = 128
PERIOD = 8


cheb_coef = (1.0, 0.45, -0.2, 0.12, -0.08)
kernel_range = 1.5


def kernel_parts(displace):
    squares = displace[0] * displace[0] + displace[1] * displace[1] + displace[2] * displace[2]
    scale_sq = kernel_range * kernel_range
    envelope = jnp.exp(squares * (-0.5 / scale_sq)) / scale_sq
    entries = []
    for left_comp in range(3):
        for right_comp in range(3):
            element = displace[left_comp] * displace[right_comp]
            if left_comp == right_comp:
                element = element - squares / 3.0
            entries.append(envelope * element)
    return jnp.stack(entries)


def phase_tables(first_ids, second_ids, length):
    product = first_ids[:, None] * second_ids[None, :] % length
    angles = product.astype(jnp.float32) * (2.0 * math.pi / length)
    return (jnp.cos(angles), jnp.sin(angles))


def signed_wave(wave_ids, length):
    return jnp.where(wave_ids < length // 2, wave_ids, wave_ids - length).astype(jnp.float32)


def per_device(noise_field, offsets, tile_list, send_cells, bead_slot, spectral):
    highest = lax.Precision.HIGHEST
    mesh_rows = lax.axis_size("row")
    row_idx = lax.axis_index("row")
    col_idx = lax.axis_index("col")
    comp_count = noise_field.shape[0]
    vec_count = noise_field.shape[1]
    row_offsets = lax.all_gather(offsets, "col", axis=1, tiled=True)
    col_offsets = lax.all_gather(offsets, "row", axis=1, tiled=True)
    row_tiles = row_offsets.shape[1] // TB
    col_tiles = col_offsets.shape[1] // TB
    tile_rows = tile_list[0, 0, 0]
    tile_cols = tile_list[0, 0, 1]
    active = tile_rows >= 0
    safe_rows = jnp.maximum(tile_rows, 0)
    safe_cols = jnp.maximum(tile_cols, 0)
    half_period = PERIOD // 2
    row_pos = row_offsets.reshape(3, row_tiles, TB)[:, safe_rows]
    col_pos = col_offsets.reshape(3, col_tiles, TB)[:, safe_cols]
    wrapped = (row_pos[:, :, :, None] - col_pos[:, :, None, :] + half_period) % PERIOD - half_period
    kernel_tiles = kernel_parts(wrapped.astype(jnp.float32)).astype(jnp.bfloat16)
    slot_count = kernel_tiles.shape[1]
    kernel_tiles = kernel_tiles.reshape(3, 3, slot_count, TB, TB)
    selector = (
        (tile_rows[:, None] == jnp.arange(row_tiles, dtype=jnp.int32)[None, :]) & active[:, None]
    ).astype(jnp.float32)
    squared = jnp.sum(jnp.square(kernel_tiles.astype(jnp.float32)), axis=(1, 4))
    energy_part = jnp.einsum("asp,si->aip", squared, selector, precision=highest).reshape(
        3, row_tiles * TB
    )

    def multiply(vector):
        gathered = lax.all_gather(vector.astype(jnp.bfloat16), "row", axis=2, tiled=True)
        pieces = gathered.reshape(comp_count, vec_count, col_tiles, TB)[:, :, safe_cols]
        blocks = jnp.einsum(
            "abspq,bksq->aksp", kernel_tiles, pieces, preferred_element_type=jnp.float32
        )
        return jnp.einsum("aksp,si->akip", blocks, selector, precision=highest).reshape(
            comp_count, vec_count, row_tiles * TB
        )

    first_sum, energy = (
        lax.psum_scatter(multiply(noise_field), "col", scatter_dimension=2, tiled=True),
        lax.psum_scatter(energy_part, "col", scatter_dimension=1, tiled=True),
    )
    largest = lax.pmax(jnp.max(energy), ("row", "col"))
    scaling = 1.0 / jnp.sqrt(largest + 1e-06)
    previous = noise_field
    current = scaling * first_sum
    near_field = cheb_coef[0] * previous + cheb_coef[1] * current
    for degree in range(2, 5):
        following = (
            2.0
            * (
                scaling
                * lax.psum_scatter(multiply(current), "col", scatter_dimension=2, tiled=True)
            )
            - previous
        )
        near_field = near_field + cheb_coef[degree] * following
        previous, current = (current, following)
    rows_x = spectral.shape[3]
    rows_y = spectral.shape[4]
    grid_len = spectral.shape[5]
    wave_x = signed_wave(row_idx * rows_x + jnp.arange(rows_x, dtype=jnp.int32), grid_len)[
        :, None, None
    ]
    wave_y = signed_wave(col_idx * rows_y + jnp.arange(rows_y, dtype=jnp.int32), grid_len)[
        None, :, None
    ]
    wave_z = signed_wave(jnp.arange(grid_len, dtype=jnp.int32), grid_len)[None, None, :]
    wave_sq = wave_x * wave_x + wave_y * wave_y + wave_z * wave_z
    width_sq = (grid_len / 8.0) ** 2
    amplitude = jnp.where(
        wave_sq > 0,
        math.sqrt(1.5) / (2.0 * math.pi * width_sq) ** 0.75 * jnp.exp(wave_sq * (-0.25 / width_sq)),
        0.0,
    )

    def project(source_field):
        along_k = wave_x * source_field[0] + wave_y * source_field[1] + wave_z * source_field[2]
        factor = along_k / jnp.maximum(wave_sq, 1.0)
        return jnp.stack(
            [
                amplitude * (source_field[0] - wave_x * factor),
                amplitude * (source_field[1] - wave_y * factor),
                amplitude * (source_field[2] - wave_z * factor),
            ]
        )

    real_part = project(spectral[0])
    imag_part = project(spectral[1])
    all_ids = jnp.arange(grid_len, dtype=jnp.int32)
    cos_full, sin_full = phase_tables(all_ids, all_ids, grid_len)

    def along_last(source_field, phase):
        return jnp.einsum("akxym,mz->akxyz", source_field, phase, precision=highest)

    section_z = jnp.stack(
        [
            along_last(real_part, cos_full) - along_last(imag_part, sin_full),
            along_last(real_part, sin_full) + along_last(imag_part, cos_full),
        ]
    )
    turned = lax.all_to_all(section_z, "col", split_axis=5, concat_axis=4, tiled=True)

    def along_y(source_field, phase):
        return jnp.einsum("akxmz,my->akxyz", source_field, phase, precision=highest)

    section_y = jnp.stack(
        [
            along_y(turned[0], cos_full) - along_y(turned[1], sin_full),
            along_y(turned[0], sin_full) + along_y(turned[1], cos_full),
        ]
    )
    y_section_slab = grid_len // mesh_rows
    slab_z = section_y.shape[5]
    slot_cap = send_cells.shape[2]
    peer_count = send_cells.shape[3]
    holder_lists = lax.all_gather(send_cells, "row", axis=0, tiled=True)
    frequency_lines = row_idx * rows_x + jnp.arange(rows_x, dtype=jnp.int32)
    flat_y = section_y.reshape(2, comp_count, vec_count, rows_x, grid_len * slab_z)
    chosen = holder_lists[:, 0]
    holders = jnp.arange(1 * lax.axis_size("row"), dtype=jnp.int32)[:, None, None]
    pos_x = (chosen // (y_section_slab * slab_z)).reshape(-1)
    pos_y = holders * y_section_slab + chosen // slab_z % y_section_slab
    pos_z = chosen % slab_z
    location_index = (pos_y * slab_z + pos_z).reshape(-1)
    values = jnp.take(flat_y, location_index, axis=4)
    cos_part, sin_part = phase_tables(frequency_lines, pos_x, grid_len)
    term_sums = jnp.sum(values[0] * cos_part - values[1] * sin_part, axis=2)
    picked = lax.psum_scatter(
        jnp.moveaxis(
            term_sums.reshape(
                comp_count, vec_count, 1 * lax.axis_size("row"), slot_cap, peer_count
            ),
            2,
            0,
        ),
        "row",
        scatter_dimension=0,
        tiled=True,
    )[0]
    arrived = lax.all_to_all(picked, ("row", "col"), split_axis=3, concat_axis=3, tiled=True)
    far_field = jnp.take(
        arrived.reshape(comp_count, vec_count, slot_cap * peer_count), bead_slot, axis=2
    )
    return near_field + far_field


def solution(mesh):
    return jax.shard_map(
        per_device,
        mesh=mesh,
        in_specs=(
            P(None, None, ("groups", "row", "col")),
            P(None, ("groups", "row", "col")),
            P(("groups", "row"), "col", None, None),
            P(("groups", "row"), "col", None, None),
            P(("groups", "row", "col")),
            P(None, None, None, ("groups", "row"), "col", None),
        ),
        out_specs=P(None, None, ("groups", "row", "col")),
        check_vma=False,
    )
```

profile of v0, /device:TPU:0, one launch (start us, length us, event | category | flops | bytes accessed | tf_op | source)
XLA Modules:
  0.0 663.8 jit_solution(7268085981516781292)
XLA Ops:
  7.7 3.9 fusion.19
  12.3 1.1 fusion.12
  13.4 3.0 fusion.5
  16.3 3.0 fusion.4
  19.3 3.0 subtract_bitcast_fusion.1
  22.3 3.2 add_bitcast_fusion.1
  25.5 3.4 pad_maximum_fusion
  28.9 20.4 %copy.151 = f32[2,3,2,32,32,128]{4,3,2,1,0,5:T(8,128)} copy(f32[2,3,2,32,32,128]{5,4,3,2,1,0:T(8,128)} %pad_maximum_fusion) | data formatting | bytes 12582912 | tf_op jit(solution)/shard_map/stack | solution.py:138
  49.3 26.8 %reshape.783 = f32[4,1,393216]{2,1,0:T(1,128)} reshape(f32[128,2,3,2,32,32]{5,4,3,2,1,0:T(8,128)} %bitcast.240) | data formatting | bytes 12582912
  76.2 6.4 all-to-all-start
  82.6 5.2 all_gather.22
  88.4 138.1 %all_gather.21 = s32[3,512]{1,0:T(4,128)S(1)} all-gather(s32[3,128]{1,0:T(4,128)S(1)} %copy-done.5), channel_id=1, replica_groups=mesh['groups'=2,'row'=4,'col'=4] {'col'}, dimensions={1}, use_global_device_ids=true | all-gather | bytes 7680 | tf_op jit(solution)/shard_map/all_gather | solution.py:47
  228.5 0.9 copy.178
  229.5 5.2 all_gather.27
  235.1 5.1 all_gather.23
  242.8 28.0 %all-reduce = f32[3,2,512]{0,1,2:T(2,128)S(1)} all-reduce(f32[3,2,512]{0,1,2:T(2,128)S(1)} %bitcast.248), channel_id=3, replica_groups=mesh['groups'=2,'row'=4,'col'=4] {'col'}, use_global_device_ids=true, to_apply=%region_5.6.clone | all-reduce | flops 3072 | bytes 24576
  271.0 3.2 fusion.30
  274.2 1.5 bitcast_reduce_fusion
  275.8 30.3 %pmax.7 = f32[]{:T(128)} all-reduce(f32[]{:T(128)} %bitcast_reduce_fusion), channel_id=1, replica_groups=mesh['groups'=2,'row'=4,'col'=4] {'row','col'}, use_global_device_ids=true, to_apply=%region_4.5 | all-reduce | flops 1 | bytes 8 | tf_op jit(solution)/shard_map/pmax | solution.py:85
  306.8 5.1 all_gather.24
  313.2 29.1 %all-reduce.1 = f32[3,2,512]{0,1,2:T(2,128)S(1)} all-reduce(f32[3,2,512]{0,1,2:T(2,128)S(1)} %bitcast.249), channel_id=4, replica_groups=mesh['groups'=2,'row'=4,'col'=4] {'col'}, use_global_device_ids=true, to_apply=%region_6.7.clone | all-reduce | flops 3072 | bytes 24576
  342.5 5.1 all_gather.25
  348.9 28.0 %all-reduce.2 = f32[3,2,512]{0,1,2:T(2,128)S(1)} all-reduce(f32[3,2,512]{0,1,2:T(2,128)S(1)} %bitcast.250), channel_id=5, replica_groups=mesh['groups'=2,'row'=4,'col'=4] {'col'}, use_global_device_ids=true, to_apply=%region_7.8.clone | all-reduce | flops 3072 | bytes 24576
  377.0 5.1 all_gather.26
  383.5 21.0 %reduce.2 = f32[4,393216]{1,0:T(4,128)} reduce(f32[4,1,393216]{2,1,0:T(1,128)} %all-to-all-done, f32[]{:T(128)} %broadcast.858), dimensions={1}, to_apply=%all_to_all.14.reduce_sub_computation | reduce | bytes 12582916 | tf_op jit(solution)/shard_map/all_to_all | solution.py:144
  404.5 19.8 %reshape.784 = f32[128,2,3,2,32,32]{5,4,3,2,1,0:T(8,128)} reshape(f32[4,393216]{1,0:T(4,128)} %reduce.2) | data formatting | bytes 12582912
  424.3 28.3 %copy.190 = f32[2,3,2,32,32,4,32]{4,5,6,3,2,1,0:T(4,128)S(1)} copy(f32[2,3,2,32,32,4,32]{4,3,2,1,0,6,5:T(8,128)} %bitcast.239) | data formatting | bytes 12582912 | tf_op jit(solution)/shard_map/all_to_all | solution.py:144
  452.6 9.0 %fusion.125 = (f32[1,3,2,32,4,32,32]{5,4,6,3,2,1,0:T(4,128)}, f32[1,3,2,32,4,32,32]{5,4,6,3,2,1,0:T(4,128)}) fusion(f32[2,3,2,32,4,32,32]{5,4,6,3,2,1,0:T(4,128)S(1)} %bitcast.238), kind=kLoop, calls=%fused_computation.234 | loop fusion | bytes 12582912 | tf_op jit(solution)/shard_map/slice | solution.py:151
  461.5 9.2 %squeeze.33 = f32[3,2,32,128,32]{3,4,2,1,0:T(8,128)S(1)} reshape(f32[1,3,2,32,4,32,32]{5,4,6,3,2,1,0:T(4,128)} %get-tuple-element.12) | data formatting | bytes 6291456 | tf_op jit(solution)/shard_map/squeeze | solution.py:151
  470.7 4.5 fusion.40
  475.2 4.5 fusion.34
  479.8 9.2 %squeeze.34 = f32[3,2,32,128,32]{3,4,2,1,0:T(8,128)S(1)} reshape(f32[1,3,2,32,4,32,32]{5,4,6,3,2,1,0:T(4,128)} %get-tuple-element.11) | data formatting | bytes 6291456 | tf_op jit(solution)/shard_map/squeeze | solution.py:151
  488.9 6.2 subtract_bitcast_fusion
  495.1 8.4 %copy.153 = f32[3,2,32,128,32]{4,3,2,1,0:T(8,128)} copy(f32[3,2,32,128,32]{3,4,2,1,0:T(8,128)} %subtract_bitcast_fusion) | data formatting | bytes 6291456 | tf_op jit(solution)/shard_map/sub | solution.py:151
  503.5 10.1 %stack.48 = f32[1,3,2,32,4096]{4,3,2,1,0:T(8,128)} reshape(f32[3,2,32,128,32]{4,3,2,1,0:T(8,128)} %copy.153) | data formatting | bytes 6291456 | tf_op jit(solution)/shard_map/stack | solution.py:149
  513.6 5.9 add_bitcast_fusion
  519.6 8.4 %copy.154 = f32[3,2,32,128,32]{4,3,2,1,0:T(8,128)} copy(f32[3,2,32,128,32]{3,4,2,1,0:T(8,128)} %add_bitcast_fusion) | data formatting | bytes 6291456 | tf_op jit(solution)/shard_map/add | solution.py:152
  527.9 10.3 %stack.49 = f32[1,3,2,32,4096]{4,3,2,1,0:T(8,128)} reshape(f32[3,2,32,128,32]{4,3,2,1,0:T(8,128)} %copy.154) | data formatting | bytes 6291456 | tf_op jit(solution)/shard_map/stack | solution.py:149
  538.2 5.1 pad_maximum_fusion.1
  543.4 30.2 %copy.155 = f32[2,3,2,32,4096]{3,2,4,1,0:T(2,128)} copy(f32[2,3,2,32,4096]{4,3,2,1,0:T(8,128)} %pad_maximum_fusion.1) | data formatting | bytes 12582912 | tf_op jit(solution)/shard_map/stack | solution.py:149
  573.6 24.9 %gather_fusion.6 = f32[1024,2,3,2,32]{4,3,2,1,0:T(2,128)} fusion(f32[2,3,2,32,4096]{3,2,4,1,0:T(2,128)} %copy.155, s32[1024]{0:T(1024)S(1)} %broadcast_clamp_fusion), kind=kCustom, calls=%fused_computation.6 | custom fusion | bytes 3149824 | tf_op jit(solution)/shard_map/jit(_take)/gather | solution.py:168
  598.5 7.1 %select_bitcast_fusion = f32[2,3,2,32,1024]{3,2,1,0,4:T(2,128)S(1)} fusion(f32[1024,2,3,2,32]{4,3,2,1,0:T(2,128)} %gather_fusion.6, pred[1024]{0:T(1024)(128)(4,1)S(1)} %compare_and_fusion), kind=kLoop, calls=%fused_computation.11 | loop fusion | flops 393216 | bytes 3146752 | tf_op jit(solution)/shard_map/jit(_take)/select_n | solution.py:168
  605.6 6.7 %fusion.2 = f32[3,2,1024]{1,0,2:T(4,128)S(1)} fusion(f32[2,3,2,32,1024]{3,2,1,0,4:T(2,128)S(1)} %select_bitcast_fusion, f32[32,1024]{0,1:T(8,128)S(1)} %copy-done.2, f32[32,1024]{0,1:T(8,128)S(1)} %copy-done.1), kind=kLoop, calls=%fused_computation.15 | loop fusion | flops 780288 | bytes 1859584 | tf_op jit(solution)/shard_map/reduce_sum | solution.py:170
  612.4 2.1 copy.157
  614.9 27.8 %all-reduce.3 = f32[3,2,512]{0,1,2:T(2,128)S(1)} all-reduce(f32[3,2,512]{0,1,2:T(2,128)S(1)} %bitcast.251), channel_id=6, replica_groups=mesh['groups'=2,'row'=4,'col'=4] {'col'}, use_global_device_ids=true, to_apply=%region_8.9.clone | all-reduce | flops 3072 | bytes 24576
  642.8 1.5 copy.158
  644.3 3.5 all-to-all-start.1
  647.9 6.4 all-to-all-done.1
  (105 shorter events, 12.9 us)
Async XLA Ops:
  7.5 4.2 slice-start
  7.7 4.6 slice-start.1
  76.2 6.5 copy-start.5
  76.2 11.6 %copy-start.6 = (s32[1,1,2,2]{3,2,1,0:T(2,128)S(1)}, s32[1,1,2,2]{3,2,1,0:T(2,128)}, u32[]{:S(2)}) copy-start(s32[1,1,2,2]{3,2,1,0:T(2,128)} %param.8) | copy-start | bytes 52
  76.2 306.8 %all-to-all-start = ((f32[4,1,393216]{2,1,0:T(1,128)}), f32[4,1,393216]{2,1,0:T(1,128)}, u32[]{:S(2)}, u32[]{:S(2)}) async-start(f32[4,1,393216]{2,1,0:T(1,128)} %reshape.783), calls=%async_computation | async-start | bytes 12582912 | tf_op jit(solution)/shard_map/all_to_all | solution.py:144
  82.6 146.9 %copy-start.4 = (s32[1,1,16,16]{3,2,1,0:T(8,128)S(1)}, s32[1,1,16,16]{3,2,1,0:T(8,128)}, u32[]{:S(2)}) copy-start(s32[1,1,16,16]{3,2,1,0:T(8,128)} %param.9) | copy-start | bytes 3076
  82.6 191.6 %reduce-scatter.7.cloned.1.call-start = ((), (), s32[]{:S(2)}) async-start(), calls=%async_computation.5 | async-start | bytes 327680
  227.0 8.1 %copy-start.3 = (f32[3,2,128]{2,1,0:T(2,128)S(1)}, f32[3,2,128]{2,1,0:T(2,128)}, u32[]{:S(2)}) copy-start(f32[3,2,128]{2,1,0:T(2,128)} %param.6) | copy-start | bytes 9220
  227.4 14.2 %copy-start.8 = (u32[32]{0:T(128)S(1)}, u32[32]{0:T(128)}, u32[]{:S(2)}) copy-start(u32[32]{0:T(128)} %constant.178) | copy-start | bytes 388
  227.5 43.3 %copy-start.7 = (s32[128]{0:T(128)S(1)}, s32[128]{0:T(128)}, u32[]{:S(2)}) copy-start(s32[128]{0:T(128)} %param.10) | copy-start | bytes 1540
  229.4 413.3 %reduce-scatter.5.cloned.1.call-start = ((), (), s32[]{:S(2)}) async-start(), calls=%async_computation.4 | async-start | bytes 245760 | tf_op jit(solution)/shard_map/reduce_scatter | solution.py:171
  527.9 10.3 %copy-start = (f32[1,3,2,32,4096]{4,3,2,1,0:T(8,128)S(1)}, f32[1,3,2,32,4096]{4,3,2,1,0:T(8,128)}, u32[]{:S(2)}) copy-start(f32[1,3,2,32,4096]{4,3,2,1,0:T(8,128)} %stack.48) | copy-start | bytes 9437188
  598.5 7.1 %copy-start.1 = (f32[32,1024]{0,1:T(8,128)S(1)}, f32[32,1024]{0,1:T(8,128)}, u32[]{:S(2)}) copy-start(f32[32,1024]{0,1:T(8,128)} %get-tuple-element.23) | copy-start | bytes 393220
  598.5 7.1 %copy-start.2 = (f32[32,1024]{0,1:T(8,128)S(1)}, f32[32,1024]{0,1:T(8,128)}, u32[]{:S(2)}) copy-start(f32[32,1024]{0,1:T(8,128)} %get-tuple-element.24) | copy-start | bytes 393220
  644.3 10.0 %all-to-all-start.1 = ((f32[3,2,16,16]{2,1,0,3:T(2,128)}), f32[3,2,16,16]{2,1,0,3:T(2,128)S(1)}, u32[]{:S(2)}, u32[]{:S(2)}) async-start(f32[3,2,16,16]{2,1,0,3:T(2,128)} %copy.158), calls=%async_computation.2 | async-start | bytes 98304 | tf_op jit(solution)/shard_map/all_to_all | solution.py:183
Sparse Core Ops, SparseCore 0:
  229.6 18.1 reduce-scatter.6
Sparse Core Ops, SparseCore 1:
  614.5 18.5 reduce-scatter.4
where the time goes:
time: 675 us; the launch traced here: 664 us
  blocking collectives  312 us (46%)
  local copies, waits for them, and re-layouts  228 us (34%)
  other arithmetic  55.4 us (8%)
  matrix products  35.4 us (5%)
  between operations  16.8 us (2%)
  starting transfers between devices  9.99 us (1%)
    all_gather x1, blocking collectives, per_device(): row_offsets = lax.all_gather(offsets, 'col', axis=1, tiled=True)  138 us
    unnamed x4, blocking collectives  113 us
    another operation x3, local copies, waits for them, and re-layouts, per_device(): jnp.stack([along_y(turned[0], cos_full) - along_y(turned[1], sin_full), a...  50.7 us
    unnamed x30, local copies, waits for them, and re-layouts  48.8 us
    pmax x1, blocking collectives, per_device(): largest = lax.pmax(jnp.max(energy), ('row', 'col'))  30.3 us
    all_to_all x2, local copies, waits for them, and re-layouts, per_device(): lax.all_to_all(section_z, 'col', split_axis=5, concat_axis=4, tiled=True)  28.8 us
    gather x1, local copies, waits for them, and re-layouts, per_device(): values = jnp.take(flat_y, location_index, axis=4)  24.9 us
    dot_general x4, matrix products, along_y(): return jnp.einsum('akxmz,my->akxyz', source_field, phase, precision=highest)  21.2 us
  transfers between devices with their start and end apart: 4, of which 1 were waited for; matrix products, arithmetic and copies ran while one was open for 2% of the time, Pallas kernels for 0%

commit v1 on v0

v1 whole, which is shorter than its diff:
```python
import functools
import math

import jax
import jax.numpy as jnp
import ml_dtypes
import numpy as np
from jax import lax
from jax.experimental import pallas as pl
from jax.experimental.pallas import tpu as pltpu
from jax.sharding import PartitionSpec as P

TB = 128
PERIOD = 8
SITES = PERIOD**3
HEAD = 16
CODE, SLOT, ROW_TILE, COL_TILE = 6, 7, 8, 9
UNIT_AXES = ("row", "col")
VMEM_BYTES = 56 * 1024 * 1024

cheb_coef = (1.0, 0.45, -0.2, 0.12, -0.08)
kernel_range = 1.5

F32 = jnp.float32
BF16 = jnp.bfloat16


def kernel_tables():
    ids = np.arange(SITES)
    coords = np.stack([ids // PERIOD**2, ids // PERIOD % PERIOD, ids % PERIOD])
    half = PERIOD // 2
    displace = (coords[:, :, None] - coords[:, None, :] + half) % PERIOD - half
    displace = displace.astype(np.float32)
    squares = (displace * displace).sum(0)
    scale_sq = np.float32(kernel_range * kernel_range)
    envelope = np.exp(squares * np.float32(-0.5 / scale_sq)) / scale_sq
    table = np.zeros((3, SITES, 3, SITES), np.float32)
    for left in range(3):
        for right in range(3):
            element = displace[left] * displace[right]
            if left == right:
                element = element - squares / np.float32(3.0)
            table[left, :, right, :] = envelope * element
    table = table.astype(ml_dtypes.bfloat16)
    squared = np.square(table.astype(np.float32)).sum(2)
    high = squared.astype(ml_dtypes.bfloat16)
    low = (squared - high.astype(np.float32)).astype(ml_dtypes.bfloat16)
    energy = np.concatenate([high, low], axis=2)
    return table.reshape(3 * SITES, 3 * SITES), energy.reshape(3 * SITES, 2 * SITES)


def wave_tables(length):
    ids = np.arange(length)
    angles = (ids[:, None] * ids[None, :] % length) * (2.0 * math.pi / length)
    return np.stack([np.cos(angles), np.sin(angles)]).astype(np.float32)


def last_transform(length):
    cos, sin = wave_tables(length)
    whole = np.concatenate(
        [np.concatenate([cos, -sin], axis=1), np.concatenate([-sin, -cos], axis=1)], axis=0
    )
    return whole.astype(ml_dtypes.bfloat16)


def split(value):
    high = value.astype(BF16)
    return high, (value - high.astype(F32)).astype(BF16)


def quotient(value, by):
    if by & (by - 1) == 0:
        return lax.shift_right_logical(value, int(math.log2(by)))
    return value // by


def remainder(value, by):
    if by & (by - 1) == 0:
        return value & (by - 1)
    return value % by


def dot_nt(left, right):
    return lax.dot_general(left, right, (((1,), (1,)), ((), ())), preferred_element_type=F32)


def dot_tn(left, right):
    return lax.dot_general(left, right, (((0,), (0,)), ((), ())), preferred_element_type=F32)


def dot(left, right):
    return jnp.dot(left, right, preferred_element_type=F32)


def lanes_from(value, start, width):
    if start % 128 == 0:
        padded = -(-width // 128) * 128
        return value[:, start : start + padded]
    total = value.shape[1]
    return pltpu.roll(value, total - start, 1)[:, : -(-width // 128) * 128]


def pack_kernel(cols, ids_ref, tiles_ref, noise_ref, offsets_ref, cells_ref, slot_ref, out_ref):
    units = out_ref.shape[0]
    slots = tiles_ref.shape[3]
    code = (offsets_ref[0:1, :] * PERIOD + offsets_ref[1:2, :]) * PERIOD + offsets_ref[2:3, :]
    lane = lax.broadcasted_iota(jnp.int32, (1, TB), 1)
    row_tile = jnp.full((1, TB), -1, jnp.int32)
    col_tile = jnp.full((1, TB), -1, jnp.int32)
    for slot in range(slots):
        tile_row = tiles_ref[0, 0, 0, slot]
        tile_col = tiles_ref[0, 0, 1, slot]
        active = tile_row >= 0
        row_unit = jnp.where(active, ids_ref[0] * cols + tile_row, -1)
        col_unit = jnp.where(active, tile_col * cols + ids_ref[1], -1)
        row_tile = jnp.where(lane == slot, row_unit, row_tile)
        col_tile = jnp.where(lane == slot, col_unit, col_tile)
    noise = jnp.concatenate([noise_ref[0], noise_ref[1], noise_ref[2]], axis=0)
    head = jnp.concatenate([code, slot_ref[...], row_tile, col_tile], axis=0).astype(F32)
    cells = cells_ref[0, 0].astype(F32)
    caps, peers = cells.shape
    out_ref[0] = jnp.zeros(out_ref.shape[1:], F32)
    out_ref[0, 0:6, :] = noise
    out_ref[0, 6:10, :] = head
    out_ref[0, HEAD : HEAD + caps, 0:peers] = cells
    block = out_ref[0]
    for unit in range(1, units):
        out_ref[unit] = block


def pack(ids, noise_field, offsets, tile_list, send_cells, bead_slot, units, cols):
    caps = send_cells.shape[2]
    rows = HEAD + -(-caps // 8) * 8
    vmem = pl.BlockSpec(memory_space=pltpu.VMEM)
    smem = pl.BlockSpec(memory_space=pltpu.SMEM)
    return pl.pallas_call(
        functools.partial(pack_kernel, cols),
        out_shape=jax.ShapeDtypeStruct((units, rows, TB), F32),
        in_specs=[smem, smem, vmem, vmem, vmem, vmem],
        out_specs=vmem,
        name="pack_inputs",
    )(ids, tile_list, noise_field, offsets, send_cells, bead_slot.reshape(1, TB))


def signed(ids, length):
    return jnp.where(ids < length // 2, ids, ids - length).astype(F32)


def spectrum_kernel(rows_x, ids_ref, spec_ref, turn_ref, out_ref):
    _, comps, vecs, part_x, rows_y, length = spec_ref.shape
    shape = (part_x, rows_y, length)
    first_x = ids_ref[0] * rows_x + pl.program_id(0) * part_x
    first_y = ids_ref[1] * rows_y
    wave = (
        signed(first_x + lax.broadcasted_iota(jnp.int32, shape, 0), length),
        signed(first_y + lax.broadcasted_iota(jnp.int32, shape, 1), length),
        signed(lax.broadcasted_iota(jnp.int32, shape, 2), length),
    )
    wave_sq = wave[0] * wave[0] + wave[1] * wave[1] + wave[2] * wave[2]
    width_sq = (length / 8.0) ** 2
    amplitude = jnp.where(
        wave_sq > 0,
        math.sqrt(1.5) / (2.0 * math.pi * width_sq) ** 0.75 * jnp.exp(wave_sq * (-0.25 / width_sq)),
        0.0,
    )
    damped = amplitude / jnp.maximum(wave_sq, 1.0)
    for vec in range(vecs):
        hat = []
        for part in range(2):
            source = [spec_ref[part, comp, vec] for comp in range(comps)]
            along = wave[0] * source[0] + wave[1] * source[1] + wave[2] * source[2]
            factor = along * damped
            hat.append(
                [
                    (amplitude * source[comp] - wave[comp] * factor)
                    .astype(BF16)
                    .reshape(part_x * rows_y, length)
                    for comp in range(comps)
                ]
            )
        for comp in range(comps):
            both = jnp.concatenate([hat[0][comp], hat[1][comp]], axis=1)
            turned = dot_nt(turn_ref[...], both).astype(BF16)
            at = (comp * vecs + vec) * length
            out_ref[0, at : at + length, :] = turned[:length]
            out_ref[1, at : at + length, :] = turned[length:]


def spectrum(ids, spectral):
    _, comps, vecs, rows_x, rows_y, length = spectral.shape
    part_x = max(1, min(rows_x, 256 // rows_y))
    while rows_x % part_x:
        part_x -= 1
    steps = rows_x // part_x
    fields = comps * vecs * length
    return pl.pallas_call(
        functools.partial(spectrum_kernel, rows_x),
        grid=(steps,),
        out_shape=jax.ShapeDtypeStruct((2, fields, rows_x * rows_y), BF16),
        in_specs=[
            pl.BlockSpec(memory_space=pltpu.SMEM),
            pl.BlockSpec((2, comps, vecs, part_x, rows_y, length), lambda i: (0, 0, 0, i, 0, 0)),
            pl.BlockSpec((2 * length, 2 * length), lambda i: (0, 0)),
        ],
        out_specs=pl.BlockSpec((2, fields, part_x * rows_y), lambda i: (0, 0, i)),
        compiler_params=pltpu.CompilerParams(vmem_limit_bytes=VMEM_BYTES),
        cost_estimate=pl.CostEstimate(
            flops=2 * 2 * fields * rows_x * rows_y * 2 * length,
            bytes_accessed=spectral.size * 4 + 4 * fields * rows_x * rows_y,
            transcendentals=rows_x * rows_y * length,
        ),
        name="spectrum",
    )(ids, spectral, jnp.asarray(last_transform(length)))


def find_cells(cols, slab_y, slab_z, packed_ref, place_ref):
    units = packed_ref.shape[0]
    caps = packed_ref.shape[1] - HEAD
    entries = units * caps
    cells = packed_ref[:, HEAD:, :].reshape(entries, TB)
    cells = jnp.transpose(cells).astype(jnp.int32)
    owners = -(-units // 16) * 16
    cells = cells[:owners]
    entry = lax.broadcasted_iota(jnp.int32, cells.shape, 1)
    holder = quotient(entry, caps)
    holder_row = quotient(holder, cols)
    holder_col = holder - holder_row * cols
    rest = quotient(cells, slab_z)
    digits = [
        quotient(rest, slab_y),
        holder_row * slab_y + remainder(rest, slab_y),
        holder_col * slab_z + remainder(cells, slab_z),
    ]
    digits = jnp.concatenate([d.astype(F32).astype(BF16) for d in digits], axis=0)
    which = lax.broadcasted_iota(jnp.int32, (entries, TB), 0)
    unit_ids = lax.broadcasted_iota(jnp.int32, (owners, TB), 0)

    def one_unit(unit, carry):
        slot = packed_ref[unit, SLOT : SLOT + 1, :].astype(jnp.int32)
        index = remainder(slot, units) * caps + quotient(slot, units)
        chosen = jnp.where(which == index, 1.0, 0.0).astype(BF16)
        found = dot(digits, chosen)
        for digit in range(3):
            rows = found[digit * owners : (digit + 1) * owners]
            place_ref[unit, digit : digit + 1, :] = jnp.sum(
                jnp.where(unit_ids == unit, rows, 0.0), axis=0, keepdims=True
            )
        return carry

    lax.fori_loop(0, units, one_unit, 0, unroll=units <= 16)


def sample_kernel(
    cols, slabs, rows, ids_ref, packed_ref, field_ref, wave_ref, out_ref, place_ref, phase_ref
):
    length = wave_ref.shape[1]
    group = out_ref.shape[0]
    fields = field_ref.shape[1] // length
    step = pl.program_id(0)

    @pl.when(step == 0)
    def _():
        find_cells(cols, slabs[0], slabs[1], packed_ref, place_ref)

    beads = group * TB
    place = [
        jnp.concatenate(
            [place_ref[step * group + unit, axis : axis + 1, :] for unit in range(group)], axis=1
        ).astype(jnp.int32)
        for axis in range(3)
    ]
    position = lax.broadcasted_iota(jnp.int32, (length, beads), 0)

    def phases(axis):
        count = rows[axis]
        first = pl.multiple_of(ids_ref[axis] * count, count)
        chosen = jnp.where(position == place[axis], 1.0, 0.0).astype(BF16)
        result = []
        for part in range(2):
            high, low = split(wave_ref[part, pl.ds(first, count), :])
            result.append(dot(high, chosen) + dot(low, chosen))
        return result

    cos_x, sin_x = phases(0)
    cos_y, sin_y = phases(1)
    rows_y = rows[1]
    for x in range(rows[0]):
        cos_one, sin_one = cos_x[x : x + 1], sin_x[x : x + 1]
        at = slice(x * rows_y, (x + 1) * rows_y)
        phase_ref[0, at, :] = (cos_one * cos_y - sin_one * sin_y).astype(BF16)
        phase_ref[1, at, :] = (cos_one * sin_y + sin_one * cos_y).astype(BF16)
    total = dot(field_ref[0], phase_ref[0]) + dot(field_ref[1], phase_ref[1])
    chosen = position == place[2]
    for field in range(fields):
        rows_z = total[field * length : (field + 1) * length]
        picked = jnp.sum(jnp.where(chosen, rows_z, 0.0), axis=0, keepdims=True)
        for unit in range(group):
            out_ref[unit, field : field + 1, :] = picked[:, unit * TB : (unit + 1) * TB]


def sample(ids, packed, field, spectral_shape, units, rows, cols):
    _, comps, vecs, rows_x, rows_y, length = spectral_shape
    group = min(4, units)
    beads = group * TB
    depth = rows_x * rows_y
    count = comps * vecs
    slabs = (length // rows, length // cols)
    return pl.pallas_call(
        functools.partial(sample_kernel, cols, slabs, (rows_x, rows_y)),
        grid=(units // group,),
        out_shape=jax.ShapeDtypeStruct((units, count, TB), F32),
        in_specs=[
            pl.BlockSpec(memory_space=pltpu.SMEM),
            pl.BlockSpec(packed.shape, lambda i: (0, 0, 0)),
            pl.BlockSpec(field.shape, lambda i: (0, 0, 0)),
            pl.BlockSpec((2, length, length), lambda i: (0, 0, 0)),
        ],
        out_specs=pl.BlockSpec((group, count, TB), lambda i: (i, 0, 0)),
        scratch_shapes=[
            pltpu.VMEM((units, 8, TB), F32),
            pltpu.VMEM((2, depth, beads), BF16),
        ],
        compiler_params=pltpu.CompilerParams(vmem_limit_bytes=VMEM_BYTES),
        cost_estimate=pl.CostEstimate(
            flops=2 * 2 * depth * count * length * units * TB,
            bytes_accessed=field.size * 2,
            transcendentals=0,
        ),
        name="sample_far",
    )(ids, packed, field, jnp.asarray(wave_tables(length)))


def near_kernel(units, slots, vecs, ids_ref, packed_ref, kernel_ref, energy_ref, out_ref):
    lanes = vecs * units
    wide = -(-lanes // 128) * 128
    fields = 3 * vecs
    copies = fields + vecs
    group = min(units, 16)
    site = lax.broadcasted_iota(jnp.int32, (SITES, TB), 0)

    lattice = None
    for first in range(0, units, group):
        held, spread = [], []
        for unit in range(first, first + group):
            code = packed_ref[unit, CODE : CODE + 1, :].astype(jnp.int32)
            held.append(jnp.where(site == code, 1.0, 0.0).astype(BF16))
            noise = packed_ref[unit, 0:fields, :]
            high, low = split(noise)
            ones = jnp.ones((vecs, TB), F32)
            pieces = jnp.concatenate(
                [high.astype(F32), ones, low.astype(F32), jnp.zeros((vecs, TB), F32)], axis=0
            )
            mine = lax.broadcasted_iota(jnp.int32, (2 * copies, units, TB), 1) == unit
            block = jnp.where(mine, pieces[:, None, :], 0.0)
            spread.append(block.reshape(2 * copies * units, TB).astype(BF16))
        part = dot_nt(jnp.concatenate(held, axis=1), jnp.concatenate(spread, axis=1))
        lattice = part if lattice is None else lattice + part
    lattice = lattice[:, : copies * units] + lattice[:, copies * units :]
    start = [lanes_from(lattice, lanes * comp, lanes) for comp in range(3)]
    count = lanes_from(lattice, lanes * 3, lanes)

    lane = lax.broadcasted_iota(jnp.int32, (units, wide), 1)
    mix = jnp.zeros((wide, wide), F32)
    row_tiles = packed_ref[:, ROW_TILE, :].astype(jnp.int32)
    col_tiles = packed_ref[:, COL_TILE, :].astype(jnp.int32)
    for slot in range(slots):
        row_unit = row_tiles[:, slot : slot + 1]
        col_unit = col_tiles[:, slot : slot + 1]
        for vec in range(vecs):
            active = row_unit >= 0
            to_row = jnp.where(active & (lane == row_unit + vec * units), 1.0, 0.0).astype(BF16)
            from_col = jnp.where(active & (lane == col_unit + vec * units), 1.0, 0.0).astype(BF16)
            mix = mix + dot_tn(from_col, to_row)
    mix = mix.astype(BF16)

    exact = count.astype(BF16)
    energy = dot(energy_ref[...], jnp.concatenate([exact, exact], axis=0))
    high, low = split(energy)
    energy = dot(high, mix) + dot(low, mix)
    valid = lax.broadcasted_iota(jnp.int32, (SITES, wide), 1) < lanes
    occupied = valid & (count > 0.5)
    largest = jnp.zeros((1, 1), F32)
    for comp in range(3):
        rows = energy[comp * SITES : (comp + 1) * SITES]
        largest = jnp.maximum(largest, jnp.max(jnp.where(occupied, rows, 0.0), keepdims=True))
    scaling = lax.rsqrt(largest + 1e-06)

    def product(vector):
        mixed = [dot(part.astype(BF16), mix).astype(BF16) for part in vector]
        whole = dot(kernel_ref[...], jnp.concatenate(mixed, axis=0))
        return [whole[comp * SITES : (comp + 1) * SITES] for comp in range(3)]

    weights = (
        cheb_coef[1] - cheb_coef[3],
        2.0 * (cheb_coef[2] - cheb_coef[4]),
        2.0 * cheb_coef[3],
        2.0 * cheb_coef[4],
    )
    previous, current = None, start
    total = None
    weight = count * scaling
    for degree in range(4):
        result = product(current)
        scaled = [weights[degree] * part for part in result]
        total = scaled if total is None else [t + s for t, s in zip(total, scaled)]
        if degree < 3:
            if previous is None:
                following = [weight * part for part in result]
            else:
                following = [2.0 * weight * r - p for r, p in zip(result, previous)]
            previous, current = current, following

    me = ids_ref[2]
    code = packed_ref[me, CODE : CODE + 1, :].astype(jnp.int32)
    held = jnp.where(site == code, 1.0, 0.0).astype(BF16)
    noise = packed_ref[me, 0:fields, :]
    row = lax.broadcasted_iota(jnp.int32, (wide, TB), 0)
    rows = []
    for comp in range(3):
        high, low = split(total[comp])
        gathered = dot_tn(high, held) + dot_tn(low, held)
        for vec in range(vecs):
            picked = jnp.where(row == vec * units + me, gathered, 0.0)
            rows.append(jnp.sum(picked, axis=0, keepdims=True))
    near = jnp.concatenate(rows, axis=0) * scaling
    out_ref[...] = (cheb_coef[0] - cheb_coef[2] + cheb_coef[4]) * noise + near


def near(ids, packed, units, slots, vecs):
    kernel_table, energy_table = kernel_tables()
    vmem = pl.BlockSpec(memory_space=pltpu.VMEM)
    return pl.pallas_call(
        functools.partial(near_kernel, units, slots, vecs),
        out_shape=jax.ShapeDtypeStruct((3 * vecs, TB), F32),
        in_specs=[pl.BlockSpec(memory_space=pltpu.SMEM), vmem, vmem, vmem],
        out_specs=vmem,
        compiler_params=pltpu.CompilerParams(vmem_limit_bytes=VMEM_BYTES),
        cost_estimate=pl.CostEstimate(
            flops=4 * 2 * 9 * SITES * SITES * 256, bytes_accessed=8 * 10**6, transcendentals=0
        ),
        name="near_field",
    )(ids, packed, jnp.asarray(kernel_table), jnp.asarray(energy_table))


def per_device(noise_field, offsets, tile_list, send_cells, bead_slot, spectral):
    rows, cols = lax.axis_size("row"), lax.axis_size("col")
    units = rows * cols
    comps, vecs, _ = noise_field.shape
    row_idx, col_idx = lax.axis_index("row"), lax.axis_index("col")
    ids = jnp.stack([row_idx, col_idx, row_idx * cols + col_idx]).astype(jnp.int32)

    def exchange(blocks):
        return lax.all_to_all(blocks, UNIT_AXES, split_axis=0, concat_axis=0, tiled=True)

    packed = exchange(
        pack(ids, noise_field, offsets, tile_list, send_cells, bead_slot, units, cols)
    )
    field = spectrum(ids, spectral)
    partial = exchange(sample(ids, packed, field, spectral.shape, units, rows, cols))
    near_field = near(ids, packed, units, tile_list.shape[3], vecs)
    velocity = near_field + jnp.sum(partial, axis=0)
    return velocity.reshape(comps, vecs, TB)


def solution(mesh):
    return jax.shard_map(
        per_device,
        mesh=mesh,
        in_specs=(
            P(None, None, ("groups", "row", "col")),
            P(None, ("groups", "row", "col")),
            P(("groups", "row"), "col", None, None),
            P(("groups", "row"), "col", None, None),
            P(("groups", "row", "col")),
            P(None, None, None, ("groups", "row"), "col", None),
        ),
        out_specs=P(None, None, ("groups", "row", "col")),
        check_vma=False,
    )
```

time: 675 us -> 55.3 us (0.08); the launches traced: 664 us -> 55 us
  blocking collectives: 312 us -> 0 us
  local copies, waits for them, and re-layouts: 228 us -> 1.28 us
  other arithmetic: 55.4 us -> 1.31 us
  Pallas kernels: 0 us -> 37.4 us
  matrix products: 35.4 us -> 0 us
  between operations: 16.8 us -> 0.02 us
    all_gather x7 -> x0, blocking collectives: 169 us -> none  [the longest x1 138 us: per_device(): row_offsets = lax.all_gather(offsets, 'col', axis=1, tiled=True)]
    unnamed x4 -> x0, blocking collectives: 113 us -> none
    another operation x4 -> x0, local copies, waits for them, and re-layouts: 71.1 us -> none  [the longest x3 50.7 us: per_device(): jnp.stack([along_y(turned[0], cos_full) - along_y(turned[1], sin_full), a...]
    unnamed x30 -> x2, local copies, waits for them, and re-layouts: 48.8 us -> 0.7 us
    pallas_call x0 -> x4, Pallas kernels: none -> 37.4 us  [the longest x1 18 us: near(): pl.pallas_call(functools.partial(near_kernel, units, slots, vecs), out_sh...]
    dot_general x17 -> x0, matrix products: 35.4 us -> none  [the longest x4 21.2 us: along_y(): return jnp.einsum('akxmz,my->akxyz', source_field, phase, precision=highest)]
    pmax x1 -> x0, blocking collectives: 30.3 us -> none  [per_device(): largest = lax.pmax(jnp.max(energy), ('row', 'col'))]
    all_to_all x3 -> x0, local copies, waits for them, and re-layouts: 29.2 us -> none  [the longest x2 28.8 us: per_device(): lax.all_to_all(section_z, 'col', split_axis=5, concat_axis=4, tiled=True)]
  transfers between devices with their start and end apart: 4 -> 2, of which waited for: 1 -> 1; matrix products, arithmetic and copies ran while one was open for 2% -> 0% of each run, Pallas kernels for 0% -> 44%
where the time goes in v1:
time: 55.3 us; the launch traced here: 55 us
  Pallas kernels  37.4 us (68%)
  starting transfers between devices  11.1 us (20%)
  waiting for transfers between devices  3.84 us (7%)
  other arithmetic  1.31 us (2%)
  local copies, waits for them, and re-layouts  1.28 us (2%)
    pallas_call x1, Pallas kernels, near(): pl.pallas_call(functools.partial(near_kernel, units, slots, vecs), out_sh...  18 us
    pallas_call x1, Pallas kernels, sample(): pl.pallas_call(functools.partial(sample_kernel, cols, slabs, (rows_x, row...  11.7 us
    all_to_all x2, starting transfers between devices, exchange(): lax.all_to_all(blocks, UNIT_AXES, split_axis=0, concat_axis=0, tiled=True)  11.1 us
    pallas_call x1, Pallas kernels, spectrum(): pl.pallas_call(functools.partial(spectrum_kernel, rows_x), grid=(steps,),...  6.23 us
    all_to_all x2, waiting for transfers between devices, exchange(): lax.all_to_all(blocks, UNIT_AXES, split_axis=0, concat_axis=0, tiled=True)  3.84 us
    pallas_call x1, Pallas kernels, pack(): pl.pallas_call(functools.partial(pack_kernel, cols), out_shape=jax.ShapeD...  1.56 us
  transfers between devices with their start and end apart: 2, of which 1 were waited for; matrix products, arithmetic and copies ran while one was open for 0% of the time, Pallas kernels for 44%

profile of v1, /device:TPU:0, one launch (start us, length us, event | category | flops | bytes accessed | tf_op | source)
XLA Modules:
  0.0 55.0 jit_solution(8343563373242021126)
XLA Ops:
  0.0 0.6 %pad_add_fusion.ids_ref = s32[3]{0:T(128)} fusion(s32[1]{0:T(128)} %bitcast.2, s32[1]{0:T(128)} %bitcast.1, s32[1]{0:T(128)} %bitcast), kind=kLoop, calls=%fused_computation | loop fusion | flops 6 | bytes 24 | tf_op jit(solution)/shard_map/stack | solution.py:450
  0.6 1.6 %pack_inputs.1 = f32[16,32,128]{2,1,0:T(8,128)} custom-call(s32[3]{0:T(128)} %pad_add_fusion.ids_ref, s32[1,1,2,2]{3,2,1,0:T(2,128)} %tiles_ref.1, f32[3,2,128]{2,1,0:T(2,128)} %noise_ref.1, s32[3,128]{1,0:T(4,128)} %offsets_ref.1, s32[1,1,16,16]{3,2,1,0:T(8,128)} %cells_ref.1, s32[1,128]{1,0:T(1,128)} %bitcast.4), custom_call_target="tpu_custom_call" | custom-call | tf_op jit(solution)/shard_map/pack_inputs/pallas_call | solution.py:136
  2.2 7.4 %all-to-all-start = ((f32[16,32,128]{2,1,0:T(8,128)}), f32[16,32,128]{2,1,0:T(8,128)S(1)}, u32[]{:S(2)}, u32[]{:S(2)}) async-start(f32[16,32,128]{2,1,0:T(8,128)} %pack_inputs.1), calls=%async_computation | async-start | bytes 524288 | tf_op jit(solution)/shard_map/all_to_all | solution.py:453
  9.6 6.2 %spectrum.1.field_ref = bf16[2,768,1024]{2,1,0:T(8,128)(2,1)} custom-call(s32[3]{0:T(128)} %pad_add_fusion.ids_ref, f32[2,3,2,32,32,128]{5,4,3,2,1,0:T(8,128)} %spec_ref.1, bf16[256,256]{1,0:T(8,128)(2,1)} %constant.19.clone.turn_ref), custom_call_target="tpu_custom_call" | custom-call | flops 805306368 | bytes 9437184 | tf_op jit(solution)/shard_map/spectrum/pallas_call | solution.py:196
  15.8 3.8 %all-to-all-done.packed_ref = f32[16,32,128]{2,1,0:T(8,128)S(1)} async-done(((f32[16,32,128]{2,1,0:T(8,128)}), f32[16,32,128]{2,1,0:T(8,128)S(1)}, u32[]{:S(2)}, u32[]{:S(2)}) %all-to-all-start) | async-done | bytes 262176 | tf_op jit(solution)/shard_map/all_to_all | solution.py:453
  19.6 0.0 copy-start
  19.6 0.7 %copy-done = f32[16,32,128]{2,1,0:T(8,128)} copy-done((f32[16,32,128]{2,1,0:T(8,128)}, f32[16,32,128]{2,1,0:T(8,128)S(1)}, u32[]{:S(2)}) %copy-start) | copy-done | bytes 262168
  20.3 11.7 %sample_far.1 = f32[16,6,128]{2,1,0:T(8,128)} custom-call(s32[3]{0:T(128)} %pad_add_fusion.ids_ref, f32[16,32,128]{2,1,0:T(8,128)} %copy-done, bf16[2,768,1024]{2,1,0:T(8,128)(2,1)} %spectrum.1.field_ref, f32[2,128,128]{2,1,0:T(8,128)} %constant.20.clone.wave_ref), custom_call_target="tpu_custom_call" | custom-call | flops 6442450944 | bytes 3145728 | tf_op jit(solution)/shard_map/sample_far/pallas_call | solution.py:308
  32.0 3.7 %all-to-all-start.1 = ((f32[16,6,128]{2,1,0:T(8,128)}), f32[16,6,128]{2,1,0:T(8,128)S(1)}, u32[]{:S(2)}, u32[]{:S(2)}) async-start(f32[16,6,128]{2,1,0:T(8,128)} %sample_far.1), calls=%async_computation.1 | async-start | bytes 131072 | tf_op jit(solution)/shard_map/all_to_all | solution.py:453
  35.7 18.0 %near_field.1 = f32[6,128]{1,0:T(8,128)} custom-call(s32[3]{0:T(128)} %pad_add_fusion.ids_ref, f32[16,32,128]{2,1,0:T(8,128)} %copy-done, bf16[1536,1536]{1,0:T(8,128)(2,1)} %constant.21.clone.kernel_ref, bf16[1536,1024]{1,0:T(8,128)(2,1)} %constant.22.clone.energy_ref), custom_call_target="tpu_custom_call" | custom-call | flops 4831838208 | bytes 8000000 | tf_op jit(solution)/shard_map/near_field/pallas_call | solution.py:432
  53.7 0.0 all-to-all-done.1
  53.7 0.7 %add.7 = f32[6,128]{1,0:T(8,128)S(1)} add(f32[6,128]{1,0:T(8,128)} %near_field.1, f32[6,128]{1,0:T(8,128)S(1)} %reduce_sum.9) | non-fusion elementwise | flops 768 | bytes 9216 | tf_op jit(solution)/shard_map/add | solution.py:461
  54.4 0.6 %reshape.7 = f32[3,2,128]{2,1,0:T(2,128)} reshape(f32[6,128]{1,0:T(8,128)S(1)} %add.7) | data formatting | bytes 6144 | tf_op jit(solution)/shard_map/reshape | solution.py:462
  (1 shorter events, 0.0 us)
Async XLA Ops:
  2.2 17.5 %all-to-all-start = ((f32[16,32,128]{2,1,0:T(8,128)}), f32[16,32,128]{2,1,0:T(8,128)S(1)}, u32[]{:S(2)}, u32[]{:S(2)}) async-start(f32[16,32,128]{2,1,0:T(8,128)} %pack_inputs.1), calls=%async_computation | async-start | bytes 524288 | tf_op jit(solution)/shard_map/all_to_all | solution.py:453
  19.6 0.7 %copy-start = (f32[16,32,128]{2,1,0:T(8,128)}, f32[16,32,128]{2,1,0:T(8,128)S(1)}, u32[]{:S(2)}) copy-start(f32[16,32,128]{2,1,0:T(8,128)S(1)} %all-to-all-done.packed_ref) | copy-start | bytes 786436
  32.0 21.7 %all-to-all-start.1 = ((f32[16,6,128]{2,1,0:T(8,128)}), f32[16,6,128]{2,1,0:T(8,128)S(1)}, u32[]{:S(2)}, u32[]{:S(2)}) async-start(f32[16,6,128]{2,1,0:T(8,128)} %sample_far.1), calls=%async_computation.1 | async-start | bytes 131072 | tf_op jit(solution)/shard_map/all_to_all | solution.py:453

commit v2 on v1

v2 whole, which is shorter than its diff:
```python
import functools
import math

import jax
import jax.numpy as jnp
import ml_dtypes
import numpy as np
from jax import lax
from jax.experimental import pallas as pl
from jax.experimental.pallas import tpu as pltpu
from jax.sharding import PartitionSpec as P

TB = 128
PERIOD = 8
SITES = PERIOD**3
OFFSETS, SLOT, ROW_TILE, COL_TILE, CELLS = 6, 9, 10, 11, 12
UNIT_AXES = ("row", "col")
VMEM_BYTES = 56 * 1024 * 1024

cheb_coef = (1.0, 0.45, -0.2, 0.12, -0.08)
kernel_range = 1.5

F32 = jnp.float32
BF16 = jnp.bfloat16


def kernel_tables():
    ids = np.arange(SITES)
    coords = np.stack([ids // PERIOD**2, ids // PERIOD % PERIOD, ids % PERIOD])
    half = PERIOD // 2
    displace = (coords[:, :, None] - coords[:, None, :] + half) % PERIOD - half
    displace = displace.astype(np.float32)
    squares = (displace * displace).sum(0)
    scale_sq = np.float32(kernel_range * kernel_range)
    envelope = np.exp(squares * np.float32(-0.5 / scale_sq)) / scale_sq
    same, other = [], []
    for left in range(3):
        right = (left + 1) % 3
        same.append(envelope * (displace[left] * displace[left] - squares / np.float32(3.0)))
        other.append(envelope * (displace[left] * displace[right]))
    same = np.stack(same).astype(ml_dtypes.bfloat16)
    other = np.stack(other).astype(ml_dtypes.bfloat16)
    squared = [np.square(t.astype(np.float32)) for t in (same, other)]
    energy = squared[0] + squared[1] + np.roll(squared[1], 1, axis=0)
    high = energy.astype(ml_dtypes.bfloat16)
    low = (energy - high.astype(np.float32)).astype(ml_dtypes.bfloat16)
    return same, other, np.concatenate([high, low], axis=2)


def wave_tables(length):
    ids = np.arange(length)
    angles = (ids[:, None] * ids[None, :] % length) * (2.0 * math.pi / length)
    return np.stack([np.cos(angles), np.sin(angles)]).astype(np.float32)


def last_transform(length):
    cos, sin = wave_tables(length)
    whole = np.concatenate(
        [np.concatenate([cos, -sin], axis=1), np.concatenate([-sin, -cos], axis=1)], axis=0
    )
    return whole.astype(ml_dtypes.bfloat16)


def split(value):
    high = value.astype(BF16)
    return high, (value - high.astype(F32)).astype(BF16)


def quotient(value, by):
    if by & (by - 1) == 0:
        return lax.shift_right_logical(value, int(math.log2(by)))
    return value // by


def remainder(value, by):
    if by & (by - 1) == 0:
        return value & (by - 1)
    return value % by


def dot_nt(left, right):
    return lax.dot_general(left, right, (((1,), (1,)), ((), ())), preferred_element_type=F32)


def dot_tn(left, right):
    return lax.dot_general(left, right, (((0,), (0,)), ((), ())), preferred_element_type=F32)


def dot(left, right):
    return jnp.dot(left, right, preferred_element_type=F32)


def pack_kernel(cols, ids_ref, tiles_ref, noise_ref, offsets_ref, cells_ref, slot_ref, out_ref):
    units = out_ref.shape[0]
    slots = tiles_ref.shape[3]
    lane = lax.broadcasted_iota(jnp.int32, (1, TB), 1)
    row_tile = jnp.full((1, TB), -1, jnp.int32)
    col_tile = jnp.full((1, TB), -1, jnp.int32)
    for slot in range(slots):
        tile_row = tiles_ref[0, 0, 0, slot]
        tile_col = tiles_ref[0, 0, 1, slot]
        active = tile_row >= 0
        row_unit = jnp.where(active, ids_ref[0] * cols + tile_row, -1)
        col_unit = jnp.where(active, tile_col * cols + ids_ref[1], -1)
        row_tile = jnp.where(lane == slot, row_unit, row_tile)
        col_tile = jnp.where(lane == slot, col_unit, col_tile)
    cells = cells_ref[0, 0].astype(F32)
    caps, peers = cells.shape
    if peers < TB:
        cells = jnp.concatenate([cells, jnp.zeros((caps, TB - peers), F32)], axis=1)
        cells = pltpu.roll(cells, 0, 1, stride=peers, stride_axis=0)
        per_row = TB // peers
        cells = jnp.concatenate(
            [
                jnp.sum(cells[at : at + per_row], axis=0, keepdims=True)
                for at in range(0, caps, per_row)
            ],
            axis=0,
        )
    head = [offsets_ref[...], slot_ref[...], row_tile, col_tile]
    block = jnp.concatenate(
        [noise_ref[0], noise_ref[1], noise_ref[2]] + [part.astype(F32) for part in head] + [cells],
        axis=0,
    )
    spare = out_ref.shape[1] - block.shape[0]
    if spare:
        block = jnp.concatenate([block, jnp.zeros((spare, TB), F32)], axis=0)
    for unit in range(units):
        out_ref[unit] = block


def cell_rows(caps, peers):
    per_row = max(1, TB // peers)
    return per_row, -(-caps // per_row)


def pack(ids, noise_field, offsets, tile_list, send_cells, bead_slot, units, cols):
    _, lists = cell_rows(*send_cells.shape[2:])
    rows = -(-(CELLS + lists) // 8) * 8
    vmem = pl.BlockSpec(memory_space=pltpu.VMEM)
    smem = pl.BlockSpec(memory_space=pltpu.SMEM)
    return pl.pallas_call(
        functools.partial(pack_kernel, cols),
        out_shape=jax.ShapeDtypeStruct((units, rows, TB), F32),
        in_specs=[smem, smem, vmem, vmem, vmem, vmem],
        out_specs=vmem,
        name="pack_inputs",
    )(ids, tile_list, noise_field, offsets, send_cells, bead_slot.reshape(1, TB))


def signed(ids, length):
    return jnp.where(ids < length // 2, ids, ids - length).astype(F32)


def spectrum_kernel(rows_x, ids_ref, spec_ref, turn_ref, out_ref):
    _, comps, vecs, part_x, rows_y, length = spec_ref.shape
    shape = (part_x, rows_y, length)
    first_x = ids_ref[0] * rows_x + pl.program_id(0) * part_x
    first_y = ids_ref[1] * rows_y
    wave = (
        signed(first_x + lax.broadcasted_iota(jnp.int32, shape, 0), length),
        signed(first_y + lax.broadcasted_iota(jnp.int32, shape, 1), length),
        signed(lax.broadcasted_iota(jnp.int32, shape, 2), length),
    )
    wave_sq = wave[0] * wave[0] + wave[1] * wave[1] + wave[2] * wave[2]
    width_sq = (length / 8.0) ** 2
    amplitude = jnp.where(
        wave_sq > 0,
        math.sqrt(1.5) / (2.0 * math.pi * width_sq) ** 0.75 * jnp.exp(wave_sq * (-0.25 / width_sq)),
        0.0,
    )
    damped = amplitude / jnp.maximum(wave_sq, 1.0)
    for vec in range(vecs):
        hat = []
        for part in range(2):
            source = [spec_ref[part, comp, vec] for comp in range(comps)]
            along = wave[0] * source[0] + wave[1] * source[1] + wave[2] * source[2]
            factor = along * damped
            hat.append(
                [
                    (amplitude * source[comp] - wave[comp] * factor)
                    .astype(BF16)
                    .reshape(part_x * rows_y, length)
                    for comp in range(comps)
                ]
            )
        for comp in range(comps):
            both = jnp.concatenate([hat[0][comp], hat[1][comp]], axis=1)
            turned = dot_nt(turn_ref[...], both).astype(BF16)
            at = (comp * vecs + vec) * length
            out_ref[0, at : at + length, :] = turned[:length]
            out_ref[1, at : at + length, :] = turned[length:]


def spectrum(ids, spectral):
    _, comps, vecs, rows_x, rows_y, length = spectral.shape
    part_x = max(1, min(rows_x, 256 // rows_y))
    while rows_x % part_x:
        part_x -= 1
    steps = rows_x // part_x
    fields = comps * vecs * length
    return pl.pallas_call(
        functools.partial(spectrum_kernel, rows_x),
        grid=(steps,),
        out_shape=jax.ShapeDtypeStruct((2, fields, rows_x * rows_y), BF16),
        in_specs=[
            pl.BlockSpec(memory_space=pltpu.SMEM),
            pl.BlockSpec((2, comps, vecs, part_x, rows_y, length), lambda i: (0, 0, 0, i, 0, 0)),
            pl.BlockSpec((2 * length, 2 * length), lambda i: (0, 0)),
        ],
        out_specs=pl.BlockSpec((2, fields, part_x * rows_y), lambda i: (0, 0, i)),
        compiler_params=pltpu.CompilerParams(vmem_limit_bytes=VMEM_BYTES),
        cost_estimate=pl.CostEstimate(
            flops=2 * 2 * fields * rows_x * rows_y * 2 * length,
            bytes_accessed=spectral.size * 4 + 4 * fields * rows_x * rows_y,
            transcendentals=rows_x * rows_y * length,
        ),
        name="spectrum",
    )(ids, spectral, jnp.asarray(last_transform(length)))


def find_cells(cols, slabs, per_row, lists, packed_ref, first, group):
    units = packed_ref.shape[0]
    entries = units * lists
    cells = packed_ref[:, CELLS : CELLS + lists, :].reshape(entries, TB).astype(jnp.int32)
    entry = lax.broadcasted_iota(jnp.int32, cells.shape, 0)
    holder = quotient(entry, lists)
    holder_row = quotient(holder, cols)
    holder_col = holder - holder_row * cols
    rest = quotient(cells, slabs[1])
    digits = [
        quotient(rest, slabs[0]),
        holder_row * slabs[0] + remainder(rest, slabs[0]),
        holder_col * slabs[1] + remainder(cells, slabs[1]),
    ]
    digits = jnp.concatenate([d.astype(F32).astype(BF16) for d in digits], axis=1)
    beads = group * TB
    slot = jnp.concatenate(
        [packed_ref[first + unit, SLOT : SLOT + 1, :] for unit in range(group)], axis=1
    ).astype(jnp.int32)
    owner = first + quotient(lax.broadcasted_iota(jnp.int32, (1, beads), 1), TB)
    order = quotient(slot, units)
    index = remainder(slot, units) * lists + quotient(order, per_row)
    lane = remainder(order, per_row) * units + owner
    chosen = lax.broadcasted_iota(jnp.int32, (entries, beads), 0) == index
    found = dot_tn(digits, jnp.where(chosen, 1.0, 0.0).astype(BF16))
    mine = lax.broadcasted_iota(jnp.int32, (TB, beads), 0) == lane
    return [
        jnp.sum(
            jnp.where(mine, found[digit * TB : (digit + 1) * TB], 0.0), axis=0, keepdims=True
        ).astype(jnp.int32)
        for digit in range(3)
    ]


def sample_kernel(
    cols, slabs, rows, lists, group, ids_ref, packed_ref, field_ref, wave_ref, out_ref, phase_ref
):
    length = wave_ref.shape[1]
    comps, vecs = out_ref.shape[1:3]
    beads = group * TB
    position = lax.broadcasted_iota(jnp.int32, (length, beads), 0)
    tables = []
    for axis in range(2):
        first = pl.multiple_of(ids_ref[axis] * rows[axis], rows[axis])
        parts = [split(wave_ref[part, pl.ds(first, rows[axis]), :]) for part in range(2)]
        tables.append(jnp.concatenate([part for pair in parts for part in pair], axis=0))
    rows_y = rows[1]

    def phases(axis, place):
        count = rows[axis]
        chosen = jnp.where(position == place, 1.0, 0.0).astype(BF16)
        found = dot(tables[axis], chosen)
        return [found[2 * p * count : (2 * p + 1) * count] + found[(2 * p + 1) * count : (2 * p + 2) * count] for p in range(2)]

    for part in range(out_ref.shape[0] // group):
        first = pl.program_id(0) * out_ref.shape[0] + part * group
        place = find_cells(cols, slabs, lists[0], lists[1], packed_ref, first, group)
        cos_x, sin_x = phases(0, place[0])
        cos_y, sin_y = [v.astype(BF16) for v in phases(1, place[1])]
        for x in range(rows[0]):
            cos_one = jnp.broadcast_to(cos_x[x : x + 1], (rows_y, beads)).astype(BF16)
            sin_one = jnp.broadcast_to(sin_x[x : x + 1], (rows_y, beads)).astype(BF16)
            at = slice(x * rows_y, (x + 1) * rows_y)
            phase_ref[part % 2, 0, at, :] = cos_one * cos_y - sin_one * sin_y
            phase_ref[part % 2, 1, at, :] = cos_one * sin_y + sin_one * cos_y
        total = dot(field_ref[0], phase_ref[part % 2, 0]) + dot(field_ref[1], phase_ref[part % 2, 1])
        chosen = position == place[2]
        for comp in range(comps):
            for vec in range(vecs):
                at = (comp * vecs + vec) * length
                picked = jnp.where(chosen, total[at : at + length], 0.0)
                picked = jnp.sum(picked, axis=0, keepdims=True)
                for unit in range(group):
                    out_ref[part * group + unit, comp, vec : vec + 1, :] = picked[
                        :, unit * TB : (unit + 1) * TB
                    ]


def sample(ids, packed, field, spectral_shape, cells_shape, rows, cols):
    _, comps, vecs, rows_x, rows_y, length = spectral_shape
    units = rows * cols
    group = 4
    whole = min(16, units)
    depth = rows_x * rows_y
    count = comps * vecs
    slabs = (length // rows, length // cols)
    lists = cell_rows(*cells_shape[2:])
    return pl.pallas_call(
        functools.partial(sample_kernel, cols, slabs, (rows_x, rows_y), lists, group),
        grid=(units // whole,),
        out_shape=jax.ShapeDtypeStruct((units, comps, vecs, TB), F32),
        in_specs=[
            pl.BlockSpec(memory_space=pltpu.SMEM),
            pl.BlockSpec(packed.shape, lambda i: (0, 0, 0)),
            pl.BlockSpec(field.shape, lambda i: (0, 0, 0)),
            pl.BlockSpec((2, length, length), lambda i: (0, 0, 0)),
        ],
        out_specs=pl.BlockSpec((whole, comps, vecs, TB), lambda i: (i, 0, 0, 0)),
        scratch_shapes=[pltpu.VMEM((2, 2, depth, group * TB), BF16)],
        compiler_params=pltpu.CompilerParams(vmem_limit_bytes=VMEM_BYTES),
        cost_estimate=pl.CostEstimate(
            flops=2 * 2 * depth * count * length * units * TB,
            bytes_accessed=field.size * 2,
            transcendentals=0,
        ),
        name="sample_far",
    )(ids, packed, field, jnp.asarray(wave_tables(length)))


def near_kernel(
    units, slots, vecs, ids_ref, packed_ref, same_hbm, other_hbm, energy_hbm, out_ref,
    same_ref, other_ref, energy_ref, rows_ref, sems,
):
    copies = [
        pltpu.make_async_copy(source, target, sems.at[at])
        for at, (source, target) in enumerate(
            [(energy_hbm, energy_ref), (same_hbm, same_ref), (other_hbm, other_ref)]
        )
    ]
    for copy in copies:
        copy.start()

    part = vecs * units
    wide = 4 * part
    fields = 3 * vecs
    group = min(units, 16)
    site = lax.broadcasted_iota(jnp.int32, (SITES, TB), 0)
    block_of = quotient(lax.broadcasted_iota(jnp.int32, (SITES, wide), 1), part)

    def sites_of(unit):
        rows = [packed_ref[unit, OFFSETS + axis : OFFSETS + axis + 1, :] for axis in range(3)]
        code = (rows[0] * PERIOD + rows[1]) * PERIOD + rows[2]
        return jnp.where(site == code.astype(jnp.int32), 1.0, 0.0).astype(BF16)

    lattice = None
    for first in range(0, units, group):
        held, spread = [], []
        for unit in range(first, first + group):
            held.append(sites_of(unit))
            high, low = split(packed_ref[unit, 0:fields, :])
            ones, zeros = jnp.ones((vecs, TB), F32), jnp.zeros((vecs, TB), F32)
            pieces = jnp.concatenate([high.astype(F32), ones, low.astype(F32), zeros], axis=0)
            mine = lax.broadcasted_iota(jnp.int32, (8 * vecs, units, TB), 1) == unit
            block = jnp.where(mine, pieces[:, None, :], 0.0)
            spread.append(block.reshape(2 * wide, TB).astype(BF16))
        term = dot_nt(jnp.concatenate(held, axis=1), jnp.concatenate(spread, axis=1))
        lattice = term if lattice is None else lattice + term
    lattice = lattice[:, :wide] + lattice[:, wide:]
    to_all = lax.broadcasted_iota(jnp.int32, (wide, wide), 0) == 3 * part + remainder(
        lax.broadcasted_iota(jnp.int32, (wide, wide), 1), units
    )
    count = dot(lattice.astype(BF16), jnp.where(to_all, 1.0, 0.0).astype(BF16))

    lane = lax.broadcasted_iota(jnp.int32, (units, wide), 1)
    row_tiles = packed_ref[:, ROW_TILE, :].astype(jnp.int32)
    col_tiles = packed_ref[:, COL_TILE, :].astype(jnp.int32)
    mix = None
    for slot in range(slots):
        row_unit = row_tiles[:, slot : slot + 1]
        col_unit = col_tiles[:, slot : slot + 1]
        active = row_unit >= 0
        from_col, to_row = [], []
        for vec in range(vecs):
            for comp in range(3):

                def hot(unit, at):
                    hit = active & (lane == unit + (at * part + vec * units))
                    return jnp.where(hit, 1.0, 0.0)

                from_col.append(hot(col_unit, comp))
                to_row.append(
                    jnp.concatenate([hot(row_unit, (comp - turn) % 3) for turn in range(3)], axis=1)
                )
        from_col = jnp.concatenate(from_col, axis=0).astype(BF16)
        term = dot_tn(from_col, jnp.concatenate(to_row, axis=0).astype(BF16))
        mix = term if mix is None else mix + term
    mix = mix.astype(BF16)
    mix = jnp.concatenate([mix, mix], axis=0)

    def in_block(block, value):
        return jnp.where(block_of == block, value, 0.0)

    copies[0].wait()
    exact = count.astype(BF16)
    exact = jnp.concatenate([exact, exact], axis=0)
    energy = sum(in_block(comp, dot(energy_ref[comp], exact)) for comp in range(3))
    energy = dot(jnp.concatenate(split(energy), axis=1), mix[:, :wide])
    occupied = (count > 0.5) & (block_of < 3)
    largest = jnp.max(jnp.where(occupied, energy, 0.0), keepdims=True)
    scaling = lax.rsqrt(largest + 1e-06)

    copies[1].wait()
    copies[2].wait()

    def product(vector):
        mixed = dot(jnp.concatenate(split(vector), axis=1), mix).astype(BF16)
        result = None
        for comp in range(3):
            same = dot(same_ref[comp], mixed[:, :wide])
            other = dot(other_ref[comp], mixed[:, wide:])
            term = in_block(comp, same + other[:, :wide]) + in_block(
                (comp + 1) % 3, other[:, wide:]
            )
            result = term if result is None else result + term
        return result

    weights = (
        cheb_coef[1] - cheb_coef[3],
        2.0 * (cheb_coef[2] - cheb_coef[4]),
        2.0 * cheb_coef[3],
        2.0 * cheb_coef[4],
    )
    weight = count * scaling
    previous, current, total = None, lattice, None
    for degree in range(4):
        result = product(current)
        scaled = weights[degree] * result
        total = scaled if total is None else total + scaled
        if degree < 3:
            following = weight * result
            if previous is not None:
                following = 2.0 * following - previous
            previous, current = current, following

    me = ids_ref[2]
    high, low = split(total)
    held = sites_of(me)
    rows_ref[...] = dot_tn(high, held) + dot_tn(low, held)
    first_weight = cheb_coef[0] - cheb_coef[2] + cheb_coef[4]
    for comp in range(3):
        for vec in range(vecs):
            near = rows_ref[pl.ds(comp * part + vec * units + me, 1), :] * scaling
            at = comp * vecs + vec
            noise = packed_ref[me, at : at + 1, :]
            out_ref[comp, vec : vec + 1, :] = first_weight * noise + near


def near(ids, packed, units, slots, vecs):
    tables = [jnp.asarray(table) for table in kernel_tables()]
    vmem = pl.BlockSpec(memory_space=pltpu.VMEM)
    hbm = pl.BlockSpec(memory_space=pl.ANY)
    return pl.pallas_call(
        functools.partial(near_kernel, units, slots, vecs),
        out_shape=jax.ShapeDtypeStruct((3, vecs, TB), F32),
        in_specs=[pl.BlockSpec(memory_space=pltpu.SMEM), vmem, hbm, hbm, hbm],
        out_specs=vmem,
        scratch_shapes=[pltpu.VMEM(table.shape, BF16) for table in tables]
        + [pltpu.VMEM((4 * vecs * units, TB), F32), pltpu.SemaphoreType.DMA((3,))],
        compiler_params=pltpu.CompilerParams(vmem_limit_bytes=VMEM_BYTES),
        cost_estimate=pl.CostEstimate(
            flops=4 * 2 * 9 * SITES * SITES * 256, bytes_accessed=8 * 10**6, transcendentals=0
        ),
        name="near_field",
    )(ids, packed, *tables)


def per_device(noise_field, offsets, tile_list, send_cells, bead_slot, spectral):
    rows, cols = lax.axis_size("row"), lax.axis_size("col")
    units = rows * cols
    vecs = noise_field.shape[1]
    row_idx, col_idx = lax.axis_index("row"), lax.axis_index("col")
    ids = jnp.stack([row_idx, col_idx, row_idx * cols + col_idx]).astype(jnp.int32)

    def exchange(blocks):
        return lax.all_to_all(blocks, UNIT_AXES, split_axis=0, concat_axis=0, tiled=True)

    packed = exchange(
        pack(ids, noise_field, offsets, tile_list, send_cells, bead_slot, units, cols)
    )
    field = spectrum(ids, spectral)
    far = sample(ids, packed, field, spectral.shape, send_cells.shape, rows, cols)
    partial = exchange(far)
    return near(ids, packed, units, tile_list.shape[3], vecs) + jnp.sum(partial, axis=0)


def solution(mesh):
    return jax.shard_map(
        per_device,
        mesh=mesh,
        in_specs=(
            P(None, None, ("groups", "row", "col")),
            P(None, ("groups", "row", "col")),
            P(("groups", "row"), "col", None, None),
            P(("groups", "row"), "col", None, None),
            P(("groups", "row", "col")),
            P(None, None, None, ("groups", "row"), "col", None),
        ),
        out_specs=P(None, None, ("groups", "row", "col")),
        check_vma=False,
    )
```

time: 55.3 us -> 44.9 us (0.81)
  Pallas kernels: 37.4 us -> 28.6 us
  waiting for transfers between devices: 3.84 us -> 1.12 us
  starting transfers between devices: 11.1 us -> 12.3 us
  local copies, waits for them, and re-layouts: 1.28 us -> 0.65 us
  other arithmetic: 1.31 us -> 1.9 us
    pallas_call x1, Pallas kernels: 18 us -> 9.55 us  [near(): pl.pallas_call(functools.partial(near_kernel, units, slots, vecs), out_sh...]
    all_to_all x2, waiting for transfers between devices: 3.84 us -> 1.12 us  [exchange(): lax.all_to_all(blocks, UNIT_AXES, split_axis=0, concat_axis=0, tiled=True)]
    all_to_all x2, starting transfers between devices: 11.1 us -> 12.3 us  [exchange(): lax.all_to_all(blocks, UNIT_AXES, split_axis=0, concat_axis=0, tiled=True)]
    reshape x1 -> x0, local copies, waits for them, and re-layouts: 0.59 us -> none  [per_device(): return velocity.reshape(comps, vecs, TB)]
    add x1, other arithmetic: 0.68 us -> 1.26 us  [per_device(): near(ids, packed, units, tile_list.shape[3], vecs)]
  transfers between devices with their start and end apart: 2 -> 2, of which waited for: 1 -> 1; matrix products, arithmetic and copies ran while one was open for 0% -> 0% of each run, Pallas kernels for 44% -> 35%
where the time goes in v2:
time: 44.9 us; the launch traced here: 44.6 us
  Pallas kernels  28.6 us (64%)
  starting transfers between devices  12.3 us (27%)
  other arithmetic  1.9 us (4%)
  waiting for transfers between devices  1.12 us (2%)
  local copies, waits for them, and re-layouts  0.65 us (1%)
    all_to_all x2, starting transfers between devices, exchange(): lax.all_to_all(blocks, UNIT_AXES, split_axis=0, concat_axis=0, tiled=True)  12.3 us
    pallas_call x1, Pallas kernels, sample(): pl.pallas_call(functools.partial(sample_kernel, cols, slabs, (rows_x, row...  11.2 us
    pallas_call x1, Pallas kernels, near(): pl.pallas_call(functools.partial(near_kernel, units, slots, vecs), out_sh...  9.55 us
    pallas_call x1, Pallas kernels, spectrum(): pl.pallas_call(functools.partial(spectrum_kernel, rows_x), grid=(steps,),...  6.23 us
    pallas_call x1, Pallas kernels, pack(): pl.pallas_call(functools.partial(pack_kernel, cols), out_shape=jax.ShapeD...  1.57 us
    add x1, other arithmetic, per_device(): near(ids, packed, units, tile_list.shape[3], vecs)  1.26 us
    all_to_all x2, waiting for transfers between devices, exchange(): lax.all_to_all(blocks, UNIT_AXES, split_axis=0, concat_axis=0, tiled=True)  1.12 us
  transfers between devices with their start and end apart: 2, of which 1 were waited for; matrix products, arithmetic and copies ran while one was open for 0% of the time, Pallas kernels for 35%

profile of v2, /device:TPU:0, one launch (start us, length us, event | category | flops | bytes accessed | tf_op | source)
XLA Modules:
  0.0 44.6 jit_solution(1428323645345198909)
XLA Ops:
  0.0 0.6 %pad_add_fusion.ids_ref = s32[3]{0:T(128)} fusion(s32[1]{0:T(128)} %bitcast.2, s32[1]{0:T(128)} %bitcast.1, s32[1]{0:T(128)} %bitcast), kind=kLoop, calls=%fused_computation | loop fusion | flops 6 | bytes 24 | tf_op jit(solution)/shard_map/stack | solution.py:483
  0.6 1.6 %pack_inputs.1 = f32[16,16,128]{2,1,0:T(8,128)} custom-call(s32[3]{0:T(128)} %pad_add_fusion.ids_ref, s32[1,1,2,2]{3,2,1,0:T(2,128)} %tiles_ref.1, f32[3,2,128]{2,1,0:T(2,128)} %noise_ref.1, s32[3,128]{1,0:T(4,128)} %offsets_ref.1, s32[1,1,16,16]{3,2,1,0:T(8,128)} %cells_ref.1, s32[1,128]{1,0:T(1,128)} %bitcast.4), custom_call_target="tpu_custom_call" | custom-call | tf_op jit(solution)/shard_map/pack_inputs/pallas_call | solution.py:142
  2.2 7.4 %all-to-all-start = ((f32[16,16,128]{2,1,0:T(8,128)}), f32[16,16,128]{2,1,0:T(8,128)S(1)}, u32[]{:S(2)}, u32[]{:S(2)}) async-start(f32[16,16,128]{2,1,0:T(8,128)} %pack_inputs.1), calls=%async_computation | async-start | bytes 262144 | tf_op jit(solution)/shard_map/all_to_all | solution.py:486
  9.6 6.2 %spectrum.1.field_ref = bf16[2,768,1024]{2,1,0:T(8,128)(2,1)} custom-call(s32[3]{0:T(128)} %pad_add_fusion.ids_ref, f32[2,3,2,32,32,128]{5,4,3,2,1,0:T(8,128)} %spec_ref.1, bf16[256,256]{1,0:T(8,128)(2,1)} %constant.21.clone.turn_ref), custom_call_target="tpu_custom_call" | custom-call | flops 805306368 | bytes 9437184 | tf_op jit(solution)/shard_map/spectrum/pallas_call | solution.py:202
  15.8 1.1 %all-to-all-done.packed_ref = f32[16,16,128]{2,1,0:T(8,128)S(1)} async-done(((f32[16,16,128]{2,1,0:T(8,128)}), f32[16,16,128]{2,1,0:T(8,128)S(1)}, u32[]{:S(2)}, u32[]{:S(2)}) %all-to-all-start) | async-done | bytes 131104 | tf_op jit(solution)/shard_map/all_to_all | solution.py:486
  16.9 0.0 copy-start
  16.9 0.6 %copy-done = f32[16,16,128]{2,1,0:T(8,128)} copy-done((f32[16,16,128]{2,1,0:T(8,128)}, f32[16,16,128]{2,1,0:T(8,128)S(1)}, u32[]{:S(2)}) %copy-start) | copy-done | bytes 131096
  17.6 11.2 %sample_far.1 = f32[16,3,2,128]{3,2,1,0:T(2,128)} custom-call(s32[3]{0:T(128)} %pad_add_fusion.ids_ref, f32[16,16,128]{2,1,0:T(8,128)} %copy-done, bf16[2,768,1024]{2,1,0:T(8,128)(2,1)} %spectrum.1.field_ref, f32[2,128,128]{2,1,0:T(8,128)} %constant.22.clone.wave_ref), custom_call_target="tpu_custom_call" | custom-call | flops 6442450944 | bytes 3145728 | tf_op jit(solution)/shard_map/sample_far/pallas_call | solution.py:309
  28.8 4.9 %all-to-all-start.1 = ((f32[16,3,2,128]{3,2,1,0:T(2,128)}), f32[16,3,2,128]{3,2,1,0:T(2,128)S(1)}, u32[]{:S(2)}, u32[]{:S(2)}) async-start(f32[16,3,2,128]{3,2,1,0:T(2,128)} %sample_far.1), calls=%async_computation.1 | async-start | bytes 98304 | tf_op jit(solution)/shard_map/all_to_all | solution.py:486
  33.7 9.6 %near_field.1 = f32[3,2,128]{2,1,0:T(2,128)} custom-call(s32[3]{0:T(128)} %pad_add_fusion.ids_ref, f32[16,16,128]{2,1,0:T(8,128)} %copy-done, bf16[3,512,512]{2,1,0:T(8,128)(2,1)} %constant.23.clone.same_hbm, bf16[3,512,512]{2,1,0:T(8,128)(2,1)} %constant.24.clone.other_hbm, bf16[3,512,1024]{2,1,0:T(8,128)(2,1)} %constant.25.clone.energy_hbm), custom_call_target="tpu_custom_call" | custom-call | flops 4831838208 | bytes 8000000 | tf_op jit(solution)/shard_map/near_field/pallas_call | solution.py:463
  43.3 0.0 all-to-all-done.1
  43.3 1.3 %add.7 = f32[3,2,128]{2,1,0:T(2,128)} add(f32[3,2,128]{2,1,0:T(2,128)} %near_field.1, f32[3,2,128]{2,1,0:T(2,128)S(1)} %reduce_sum.9) | non-fusion elementwise | flops 768 | bytes 9216 | tf_op jit(solution)/shard_map/add | solution.py:494
  (1 shorter events, 0.0 us)
Async XLA Ops:
  2.2 14.7 %all-to-all-start = ((f32[16,16,128]{2,1,0:T(8,128)}), f32[16,16,128]{2,1,0:T(8,128)S(1)}, u32[]{:S(2)}, u32[]{:S(2)}) async-start(f32[16,16,128]{2,1,0:T(8,128)} %pack_inputs.1), calls=%async_computation | async-start | bytes 262144 | tf_op jit(solution)/shard_map/all_to_all | solution.py:486
  16.9 0.6 %copy-start = (f32[16,16,128]{2,1,0:T(8,128)}, f32[16,16,128]{2,1,0:T(8,128)S(1)}, u32[]{:S(2)}) copy-start(f32[16,16,128]{2,1,0:T(8,128)S(1)} %all-to-all-done.packed_ref) | copy-start | bytes 393220
  28.8 14.5 %all-to-all-start.1 = ((f32[16,3,2,128]{3,2,1,0:T(2,128)}), f32[16,3,2,128]{3,2,1,0:T(2,128)S(1)}, u32[]{:S(2)}, u32[]{:S(2)}) async-start(f32[16,3,2,128]{3,2,1,0:T(2,128)} %sample_far.1), calls=%async_computation.1 | async-start | bytes 98304 | tf_op jit(solution)/shard_map/all_to_all | solution.py:486

commit v3 on v2

--- a/solution.py
+++ b/solution.py
@@ -13,9 +13,12 @@
 TB = 128
 PERIOD = 8
 SITES = PERIOD**3
+PLANE = PERIOD**2
+WINDOW = SITES + (PERIOD - 2) * PLANE
 OFFSETS, SLOT, ROW_TILE, COL_TILE, CELLS = 6, 9, 10, 11, 12
 UNIT_AXES = ("row", "col")
-VMEM_BYTES = 56 * 1024 * 1024
+MIB = 1024 * 1024
+SPECTRUM_BYTES, SAMPLE_BYTES, NEAR_BYTES = 28 * MIB, 28 * MIB, 28 * MIB
 
 cheb_coef = (1.0, 0.45, -0.2, 0.12, -0.08)
 kernel_range = 1.5
@@ -28,7 +31,9 @@
     ids = np.arange(SITES)
     coords = np.stack([ids // PERIOD**2, ids // PERIOD % PERIOD, ids % PERIOD])
     half = PERIOD // 2
-    displace = (coords[:, :, None] - coords[:, None, :] + half) % PERIOD - half
+    starts = np.stack([np.arange(WINDOW), np.arange(WINDOW) + PLANE])
+    columns = coords[:, starts % SITES]
+    displace = (coords[:, None, :PLANE, None] - columns[:, :, None, :] + half) % PERIOD - half
     displace = displace.astype(np.float32)
     squares = (displace * displace).sum(0)
     scale_sq = np.float32(kernel_range * kernel_range)
@@ -44,7 +49,16 @@
     energy = squared[0] + squared[1] + np.roll(squared[1], 1, axis=0)
     high = energy.astype(ml_dtypes.bfloat16)
     low = (energy - high.astype(np.float32)).astype(ml_dtypes.bfloat16)
-    return same, other, np.concatenate([high, low], axis=2)
+    return np.stack([same, other]), np.stack([high, low])
+
+
+def whole_table(ref, kind, comp):
+    blocks = []
+    for first in range(PERIOD):
+        start = -first % PERIOD
+        column = (start - start % 2) * PLANE
+        blocks.append(ref[kind, comp, start % 2, :, column : column + SITES])
+    return jnp.concatenate(blocks, axis=0)
 
 
 def wave_tables(length):
@@ -90,9 +104,14 @@
     return jnp.dot(left, right, preferred_element_type=F32)
 
 
-def pack_kernel(cols, ids_ref, tiles_ref, noise_ref, offsets_ref, cells_ref, slot_ref, out_ref):
+def in_hbm(arrays):
+    return [pltpu.with_memory_space_constraint(jnp.asarray(a), pltpu.HBM) for a in arrays]
+
+
+def pack_kernel(cols, tiles_ref, noise_ref, offsets_ref, cells_ref, slot_ref, out_ref):
     units = out_ref.shape[0]
     slots = tiles_ref.shape[3]
+    my_row, my_col = lax.axis_index("row"), lax.axis_index("col")
     lane = lax.broadcasted_iota(jnp.int32, (1, TB), 1)
     row_tile = jnp.full((1, TB), -1, jnp.int32)
     col_tile = jnp.full((1, TB), -1, jnp.int32)
@@ -100,8 +119,8 @@
         tile_row = tiles_ref[0, 0, 0, slot]
         tile_col = tiles_ref[0, 0, 1, slot]
         active = tile_row >= 0
-        row_unit = jnp.where(active, ids_ref[0] * cols + tile_row, -1)
-        col_unit = jnp.where(active, tile_col * cols + ids_ref[1], -1)
+        row_unit = jnp.where(active, my_row * cols + tile_row, -1)
+        col_unit = jnp.where(active, tile_col * cols + my_col, -1)
         row_tile = jnp.where(lane == slot, row_unit, row_tile)
         col_tile = jnp.where(lane == slot, col_unit, col_tile)
     cells = cells_ref[0, 0].astype(F32)
@@ -134,7 +153,7 @@
     return per_row, -(-caps // per_row)
 
 
-def pack(ids, noise_field, offsets, tile_list, send_cells, bead_slot, units, cols):
+def pack(noise_field, offsets, tile_list, send_cells, bead_slot, units, cols):
     _, lists = cell_rows(*send_cells.shape[2:])
     rows = -(-(CELLS + lists) // 8) * 8
     vmem = pl.BlockSpec(memory_space=pltpu.VMEM)
@@ -142,81 +161,121 @@
     return pl.pallas_call(
         functools.partial(pack_kernel, cols),
         out_shape=jax.ShapeDtypeStruct((units, rows, TB), F32),
-        in_specs=[smem, smem, vmem, vmem, vmem, vmem],
+        in_specs=[smem, vmem, vmem, vmem, vmem],
         out_specs=vmem,
         name="pack_inputs",
-    )(ids, tile_list, noise_field, offsets, send_cells, bead_slot.reshape(1, TB))
+    )(tile_list, noise_field, offsets, send_cells, bead_slot.reshape(1, TB))
 
 
 def signed(ids, length):
     return jnp.where(ids < length // 2, ids, ids - length).astype(F32)
 
 
-def spectrum_kernel(rows_x, ids_ref, spec_ref, turn_ref, out_ref):
-    _, comps, vecs, part_x, rows_y, length = spec_ref.shape
+def spectrum_kernel(
+    rows_x, spec_hbm, turn_hbm, wave_hbm, out_ref, phase_ref, spec_ref, turn_ref, wave_ref, sems
+):
+    steps, _, comps, vecs, part_x, rows_y, length = spec_ref.shape
+    depth = part_x * rows_y
     shape = (part_x, rows_y, length)
-    first_x = ids_ref[0] * rows_x + pl.program_id(0) * part_x
-    first_y = ids_ref[1] * rows_y
-    wave = (
-        signed(first_x + lax.broadcasted_iota(jnp.int32, shape, 0), length),
-        signed(first_y + lax.broadcasted_iota(jnp.int32, shape, 1), length),
-        signed(lax.broadcasted_iota(jnp.int32, shape, 2), length),
-    )
-    wave_sq = wave[0] * wave[0] + wave[1] * wave[1] + wave[2] * wave[2]
+    copies = [
+        pltpu.make_async_copy(
+            spec_hbm.at[:, :, :, pl.ds(step * part_x, part_x)], spec_ref.at[step], sems.at[step]
+        )
+        for step in range(steps)
+    ]
+    tables = [
+        pltpu.make_async_copy(source, target, sems.at[steps + at])
+        for at, (source, target) in enumerate(
+            [(turn_hbm, turn_ref), (wave_hbm, wave_ref)]
+        )
+    ]
+    copies[0].start()
+    tables[0].start()
+    for copy in copies[1:] + tables[1:]:
+        copy.start()
+    wave_y = signed(lax.axis_index("col") * rows_y + lax.broadcasted_iota(jnp.int32, shape, 1), length)
+    wave_z = signed(lax.broadcasted_iota(jnp.int32, shape, 2), length)
     width_sq = (length / 8.0) ** 2
-    amplitude = jnp.where(
-        wave_sq > 0,
-        math.sqrt(1.5) / (2.0 * math.pi * width_sq) ** 0.75 * jnp.exp(wave_sq * (-0.25 / width_sq)),
-        0.0,
-    )
-    damped = amplitude / jnp.maximum(wave_sq, 1.0)
-    for vec in range(vecs):
-        hat = []
-        for part in range(2):
-            source = [spec_ref[part, comp, vec] for comp in range(comps)]
-            along = wave[0] * source[0] + wave[1] * source[1] + wave[2] * source[2]
-            factor = along * damped
-            hat.append(
-                [
-                    (amplitude * source[comp] - wave[comp] * factor)
-                    .astype(BF16)
-                    .reshape(part_x * rows_y, length)
-                    for comp in range(comps)
-                ]
-            )
-        for comp in range(comps):
-            both = jnp.concatenate([hat[0][comp], hat[1][comp]], axis=1)
-            turned = dot_nt(turn_ref[...], both).astype(BF16)
-            at = (comp * vecs + vec) * length
-            out_ref[0, at : at + length, :] = turned[:length]
-            out_ref[1, at : at + length, :] = turned[length:]
-
-
-def spectrum(ids, spectral):
-    _, comps, vecs, rows_x, rows_y, length = spectral.shape
+    height = math.sqrt(1.5) / (2.0 * math.pi * width_sq) ** 0.75
+    for step in range(steps):
+        first_x = lax.axis_index("row") * rows_x + step * part_x
+        wave_x = signed(first_x + lax.broadcasted_iota(jnp.int32, shape, 0), length)
+        wave = (wave_x, wave_y, wave_z)
+        wave_sq = wave_x * wave_x + wave_y * wave_y + wave_z * wave_z
+        amplitude = height * jnp.exp(wave_sq * (-0.25 / width_sq))
+        amplitude = jnp.where(wave_sq > 0, amplitude, 0.0)
+        damped = amplitude / jnp.maximum(wave_sq, 1.0)
+        copies[step].wait()
+        if step == 0:
+            tables[0].wait()
+        for vec in range(vecs):
+            hat = []
+            for part in range(2):
+                source = [spec_ref[step, part, comp, vec] for comp in range(comps)]
+                along = wave_x * source[0] + wave_y * source[1] + wave_z * source[2]
+                factor = along * damped
+                hat.append(
+                    [
+                        (amplitude * source[comp] - wave[comp] * factor)
+                        .astype(BF16)
+                        .reshape(depth, length)
+                        for comp in range(comps)
+                    ]
+                )
+            for comp in range(comps):
+                both = jnp.concatenate([hat[0][comp], hat[1][comp]], axis=1)
+                turned = dot_nt(turn_ref[...], both).astype(BF16)
+                at = (comp * vecs + vec) * length
+                column = 2 * step * depth
+                out_ref[at : at + length, column : column + depth] = turned[:length]
+                column += depth
+                out_ref[at : at + length, column : column + depth] = turned[length:]
+    for table in tables[1:]:
+        table.wait()
+    for axis, count in enumerate((rows_x, rows_y)):
+        first = pl.multiple_of(lax.axis_index(UNIT_AXES[axis]) * count, count)
+        parts = [split(wave_ref[part, pl.ds(first, count), :]) for part in range(2)]
+        parts = [piece for pair in parts for piece in pair]
+        phase_ref[axis, 0 : 4 * count, :] = jnp.concatenate(parts, axis=0)
+
+
+def chunk_of(rows_x, rows_y):
     part_x = max(1, min(rows_x, 256 // rows_y))
     while rows_x % part_x:
         part_x -= 1
+    return part_x
+
+
+def spectrum(spectral):
+    _, comps, vecs, rows_x, rows_y, length = spectral.shape
+    part_x = chunk_of(rows_x, rows_y)
     steps = rows_x // part_x
     fields = comps * vecs * length
+    sources = [spectral, last_transform(length), wave_tables(length)]
+    hbm = pl.BlockSpec(memory_space=pltpu.HBM)
+    vmem = pl.BlockSpec(memory_space=pltpu.VMEM)
     return pl.pallas_call(
         functools.partial(spectrum_kernel, rows_x),
-        grid=(steps,),
-        out_shape=jax.ShapeDtypeStruct((2, fields, rows_x * rows_y), BF16),
-        in_specs=[
-            pl.BlockSpec(memory_space=pltpu.SMEM),
-            pl.BlockSpec((2, comps, vecs, part_x, rows_y, length), lambda i: (0, 0, 0, i, 0, 0)),
-            pl.BlockSpec((2 * length, 2 * length), lambda i: (0, 0)),
+        out_shape=[
+            pltpu.VMEM((fields, 2 * rows_x * rows_y), BF16),
+            pltpu.VMEM((2, 4 * max(rows_x, rows_y), length), BF16),
         ],
-        out_specs=pl.BlockSpec((2, fields, part_x * rows_y), lambda i: (0, 0, i)),
-        compiler_params=pltpu.CompilerParams(vmem_limit_bytes=VMEM_BYTES),
+        in_specs=[hbm] * 3,
+        out_specs=[vmem] * 2,
+        scratch_shapes=[
+            pltpu.VMEM((steps, 2, comps, vecs, part_x, rows_y, length), F32),
+            pltpu.VMEM((2 * length, 2 * length), BF16),
+            pltpu.VMEM((2, length, length), F32),
+            pltpu.SemaphoreType.DMA((steps + 2,)),
+        ],
+        compiler_params=pltpu.CompilerParams(vmem_limit_bytes=SPECTRUM_BYTES),
         cost_estimate=pl.CostEstimate(
             flops=2 * 2 * fields * rows_x * rows_y * 2 * length,
             bytes_accessed=spectral.size * 4 + 4 * fields * rows_x * rows_y,
             transcendentals=rows_x * rows_y * length,
         ),
         name="spectrum",
-    )(ids, spectral, jnp.asarray(last_transform(length)))
+    )(*in_hbm(sources))
 
 
 def find_cells(cols, slabs, per_row, lists, packed_ref, first, group):
@@ -254,93 +313,99 @@
 
 
 def sample_kernel(
-    cols, slabs, rows, lists, group, ids_ref, packed_ref, field_ref, wave_ref, out_ref, phase_ref
+    cols, slabs, rows, lists, groups, packed_ref, field_ref, table_ref, out_ref, *phase_refs
 ):
-    length = wave_ref.shape[1]
+    length = table_ref.shape[2]
     comps, vecs = out_ref.shape[1:3]
-    beads = group * TB
-    position = lax.broadcasted_iota(jnp.int32, (length, beads), 0)
-    tables = []
-    for axis in range(2):
-        first = pl.multiple_of(ids_ref[axis] * rows[axis], rows[axis])
-        parts = [split(wave_ref[part, pl.ds(first, rows[axis]), :]) for part in range(2)]
-        tables.append(jnp.concatenate([part for pair in parts for part in pair], axis=0))
     rows_y = rows[1]
+    part_x = chunk_of(*rows)
+    depth = 2 * part_x * rows_y
+
+    def hits(place):
+        position = lax.broadcasted_iota(jnp.int32, (length, place.shape[1]), 0)
+        return position == place
 
     def phases(axis, place):
         count = rows[axis]
-        chosen = jnp.where(position == place, 1.0, 0.0).astype(BF16)
-        found = dot(tables[axis], chosen)
-        return [found[2 * p * count : (2 * p + 1) * count] + found[(2 * p + 1) * count : (2 * p + 2) * count] for p in range(2)]
-
-    for part in range(out_ref.shape[0] // group):
-        first = pl.program_id(0) * out_ref.shape[0] + part * group
+        found = dot(table_ref[axis, 0 : 4 * count, :], jnp.where(hits(place), 1.0, 0.0).astype(BF16))
+        found = [found[at * count : (at + 1) * count] for at in range(4)]
+        return found[0] + found[1], found[2] + found[3]
+
+    def fill(first, group, phase_ref):
+        first = pl.program_id(0) * out_ref.shape[0] + first
+        beads = group * TB
         place = find_cells(cols, slabs, lists[0], lists[1], packed_ref, first, group)
         cos_x, sin_x = phases(0, place[0])
         cos_y, sin_y = [v.astype(BF16) for v in phases(1, place[1])]
         for x in range(rows[0]):
             cos_one = jnp.broadcast_to(cos_x[x : x + 1], (rows_y, beads)).astype(BF16)
             sin_one = jnp.broadcast_to(sin_x[x : x + 1], (rows_y, beads)).astype(BF16)
-            at = slice(x * rows_y, (x + 1) * rows_y)
-            phase_ref[part % 2, 0, at, :] = cos_one * cos_y - sin_one * sin_y
-            phase_ref[part % 2, 1, at, :] = cos_one * sin_y + sin_one * cos_y
-        total = dot(field_ref[0], phase_ref[part % 2, 0]) + dot(field_ref[1], phase_ref[part % 2, 1])
-        chosen = position == place[2]
+            at = x // part_x * depth + x % part_x * rows_y
+            phase_ref[at : at + rows_y, :] = cos_one * cos_y - sin_one * sin_y
+            at += depth // 2
+            phase_ref[at : at + rows_y, :] = cos_one * sin_y + sin_one * cos_y
+        return place[2]
+
+    def finish(first, group, total, place_z):
+        chosen = hits(place_z)
         for comp in range(comps):
             for vec in range(vecs):
                 at = (comp * vecs + vec) * length
                 picked = jnp.where(chosen, total[at : at + length], 0.0)
                 picked = jnp.sum(picked, axis=0, keepdims=True)
                 for unit in range(group):
-                    out_ref[part * group + unit, comp, vec : vec + 1, :] = picked[
+                    out_ref[first + unit, comp, vec : vec + 1, :] = picked[
                         :, unit * TB : (unit + 1) * TB
                     ]
 
-
-def sample(ids, packed, field, spectral_shape, cells_shape, rows, cols):
+    starts = [sum(groups[:at]) for at in range(len(groups))]
+    place_z = fill(0, groups[0], phase_refs[0])
+    for at, group in enumerate(groups):
+        later = None
+        if at + 1 < len(groups):
+            later = fill(starts[at + 1], groups[at + 1], phase_refs[at + 1])
+        total = dot(field_ref[...], phase_refs[at][...])
+        finish(starts[at], group, total, place_z)
+        place_z = later
+
+
+def sample(packed, field, table, spectral_shape, cells_shape, rows, cols):
     _, comps, vecs, rows_x, rows_y, length = spectral_shape
     units = rows * cols
-    group = 4
-    whole = min(16, units)
+    groups = (2, 6, 8) if units % 16 == 0 else (units,)
+    whole = sum(groups)
     depth = rows_x * rows_y
     count = comps * vecs
     slabs = (length // rows, length // cols)
     lists = cell_rows(*cells_shape[2:])
+    vmem = pl.BlockSpec(memory_space=pltpu.VMEM)
     return pl.pallas_call(
-        functools.partial(sample_kernel, cols, slabs, (rows_x, rows_y), lists, group),
+        functools.partial(sample_kernel, cols, slabs, (rows_x, rows_y), lists, groups),
         grid=(units // whole,),
         out_shape=jax.ShapeDtypeStruct((units, comps, vecs, TB), F32),
-        in_specs=[
-            pl.BlockSpec(memory_space=pltpu.SMEM),
-            pl.BlockSpec(packed.shape, lambda i: (0, 0, 0)),
-            pl.BlockSpec(field.shape, lambda i: (0, 0, 0)),
-            pl.BlockSpec((2, length, length), lambda i: (0, 0, 0)),
-        ],
+        in_specs=[vmem, vmem, vmem],
         out_specs=pl.BlockSpec((whole, comps, vecs, TB), lambda i: (i, 0, 0, 0)),
-        scratch_shapes=[pltpu.VMEM((2, 2, depth, group * TB), BF16)],
-        compiler_params=pltpu.CompilerParams(vmem_limit_bytes=VMEM_BYTES),
+        scratch_shapes=[pltpu.VMEM((2 * depth, group * TB), BF16) for group in groups],
+        compiler_params=pltpu.CompilerParams(vmem_limit_bytes=SAMPLE_BYTES),
         cost_estimate=pl.CostEstimate(
             flops=2 * 2 * depth * count * length * units * TB,
             bytes_accessed=field.size * 2,
             transcendentals=0,
         ),
         name="sample_far",
-    )(ids, packed, field, jnp.asarray(wave_tables(length)))
+    )(packed, field, table)
 
 
 def near_kernel(
-    units, slots, vecs, ids_ref, packed_ref, same_hbm, other_hbm, energy_hbm, out_ref,
-    same_ref, other_ref, energy_ref, rows_ref, sems,
+    units, cols, slots, vecs, packed_ref, table_hbm, energy_hbm, out_ref,
+    table_ref, energy_ref, rows_ref, sems,
 ):
     copies = [
-        pltpu.make_async_copy(source, target, sems.at[at])
-        for at, (source, target) in enumerate(
-            [(energy_hbm, energy_ref), (same_hbm, same_ref), (other_hbm, other_ref)]
-        )
+        pltpu.make_async_copy(table_hbm, table_ref, sems.at[0]),
+        pltpu.make_async_copy(energy_hbm, energy_ref, sems.at[1]),
     ]
     for copy in copies:
         copy.start()
-
     part = vecs * units
     wide = 4 * part
     fields = 3 * vecs
@@ -401,24 +466,25 @@
     def in_block(block, value):
         return jnp.where(block_of == block, value, 0.0)
 
-    copies[0].wait()
+    for copy in copies:
+        copy.wait()
+
     exact = count.astype(BF16)
-    exact = jnp.concatenate([exact, exact], axis=0)
-    energy = sum(in_block(comp, dot(energy_ref[comp], exact)) for comp in range(3))
+    energy = sum(
+        in_block(comp, sum(dot(whole_table(energy_ref, kind, comp), exact) for kind in range(2)))
+        for comp in range(3)
+    )
     energy = dot(jnp.concatenate(split(energy), axis=1), mix[:, :wide])
     occupied = (count > 0.5) & (block_of < 3)
     largest = jnp.max(jnp.where(occupied, energy, 0.0), keepdims=True)
     scaling = lax.rsqrt(largest + 1e-06)
 
-    copies[1].wait()
-    copies[2].wait()
-
     def product(vector):
         mixed = dot(jnp.concatenate(split(vector), axis=1), mix).astype(BF16)
         result = None
         for comp in range(3):
-            same = dot(same_ref[comp], mixed[:, :wide])
-            other = dot(other_ref[comp], mixed[:, wide:])
+            same = dot(whole_table(table_ref, 0, comp), mixed[:, :wide])
+            other = dot(whole_table(table_ref, 1, comp), mixed[:, wide:])
             term = in_block(comp, same + other[:, :wide]) + in_block(
                 (comp + 1) % 3, other[:, wide:]
             )
@@ -443,7 +509,7 @@
                 following = 2.0 * following - previous
             previous, current = current, following
 
-    me = ids_ref[2]
+    me = lax.axis_index("row") * cols + lax.axis_index("col")
     high, low = split(total)
     held = sites_of(me)
     rows_ref[...] = dot_tn(high, held) + dot_tn(low, held)
@@ -456,42 +522,41 @@
             out_ref[comp, vec : vec + 1, :] = first_weight * noise + near
 
 
-def near(ids, packed, units, slots, vecs):
-    tables = [jnp.asarray(table) for table in kernel_tables()]
+def near(packed, units, cols, slots, vecs):
+    tables = kernel_tables()
     vmem = pl.BlockSpec(memory_space=pltpu.VMEM)
-    hbm = pl.BlockSpec(memory_space=pl.ANY)
+    hbm = pl.BlockSpec(memory_space=pltpu.HBM)
     return pl.pallas_call(
-        functools.partial(near_kernel, units, slots, vecs),
-        out_shape=jax.ShapeDtypeStruct((3, vecs, TB), F32),
-        in_specs=[pl.BlockSpec(memory_space=pltpu.SMEM), vmem, hbm, hbm, hbm],
+        functools.partial(near_kernel, units, cols, slots, vecs),
+        out_shape=pltpu.VMEM((3, vecs, TB), F32),
+        in_specs=[vmem] + [hbm] * 2,
         out_specs=vmem,
         scratch_shapes=[pltpu.VMEM(table.shape, BF16) for table in tables]
-        + [pltpu.VMEM((4 * vecs * units, TB), F32), pltpu.SemaphoreType.DMA((3,))],
-        compiler_params=pltpu.CompilerParams(vmem_limit_bytes=VMEM_BYTES),
+        + [pltpu.VMEM((4 * vecs * units, TB), F32), pltpu.SemaphoreType.DMA((2,))],
+        compiler_params=pltpu.CompilerParams(vmem_limit_bytes=NEAR_BYTES),
         cost_estimate=pl.CostEstimate(
             flops=4 * 2 * 9 * SITES * SITES * 256, bytes_accessed=8 * 10**6, transcendentals=0
         ),
         name="near_field",
-    )(ids, packed, *tables)
+    )(packed, *in_hbm(tables))
 
 
 def per_device(noise_field, offsets, tile_list, send_cells, bead_slot, spectral):
     rows, cols = lax.axis_size("row"), lax.axis_size("col")
     units = rows * cols
     vecs = noise_field.shape[1]
-    row_idx, col_idx = lax.axis_index("row"), lax.axis_index("col")
-    ids = jnp.stack([row_idx, col_idx, row_idx * cols + col_idx]).astype(jnp.int32)
 
     def exchange(blocks):
         return lax.all_to_all(blocks, UNIT_AXES, split_axis=0, concat_axis=0, tiled=True)
 
     packed = exchange(
-        pack(ids, noise_field, offsets, tile_list, send_cells, bead_slot, units, cols)
-    )
-    field = spectrum(ids, spectral)
-    far = sample(ids, packed, field, spectral.shape, send_cells.shape, rows, cols)
+        pack(noise_field, offsets, tile_list, send_cells, bead_slot, units, cols)
+    )
+    field, waves = spectrum(spectral)
+    far = sample(packed, field, waves, spectral.shape, send_cells.shape, rows, cols)
     partial = exchange(far)
-    return near(ids, packed, units, tile_list.shape[3], vecs) + jnp.sum(partial, axis=0)
+    near_field = near(packed, units, cols, tile_list.shape[3], vecs)
+    return near_field + jnp.sum(partial, axis=0)
 
 
 def solution(mesh):

time: 44.9 us -> 37 us (0.82)
  Pallas kernels: 28.6 us -> 21.3 us
  waiting for transfers between devices: 1.12 us -> 3.69 us
  other arithmetic: 1.9 us -> 0.62 us
  starting transfers between devices: 12.3 us -> 11.1 us
  local copies, waits for them, and re-layouts: 0.65 us -> 0 us
    pallas_call x2, Pallas kernels: 15.8 us -> 11.3 us  [the longest x1 7.66 us: near(): pl.pallas_call(functools.partial(near_kernel, units, cols, slots, vecs),...]
    pallas_call x1, Pallas kernels: 11.2 us -> 8.41 us  [sample(): pl.pallas_call(functools.partial(sample_kernel, cols, slabs, (rows_x, row...]
    all_to_all x2, waiting for transfers between devices: 1.12 us -> 3.69 us  [exchange(): lax.all_to_all(blocks, UNIT_AXES, split_axis=0, concat_axis=0, tiled=True)]
    all_to_all x2, starting transfers between devices: 12.3 us -> 11.1 us  [exchange(): lax.all_to_all(blocks, UNIT_AXES, split_axis=0, concat_axis=0, tiled=True)]
    add x1, other arithmetic: 1.26 us -> 0.58 us  [per_device(): return near_field + jnp.sum(partial, axis=0)]
    unnamed x2 -> x0, local copies, waits for them, and re-layouts: 0.65 us -> none
    another operation x1 -> x0, other arithmetic: 0.6 us -> none  [per_device(): jnp.stack([row_idx, col_idx, row_idx * cols + col_idx]).astype(jnp.int32)]
  transfers between devices with their start and end apart: 2 -> 2, of which waited for: 1 -> 1; matrix products, arithmetic and copies ran while one was open for 0% -> 0% of each run, Pallas kernels for 35% -> 31%
where the time goes in v3:
time: 37 us; the launch traced here: 36.7 us
  Pallas kernels  21.3 us (58%)
  starting transfers between devices  11.1 us (30%)
  waiting for transfers between devices  3.69 us (10%)
  other arithmetic  0.62 us (2%)
    all_to_all x2, starting transfers between devices, exchange(): lax.all_to_all(blocks, UNIT_AXES, split_axis=0, concat_axis=0, tiled=True)  11.1 us
    pallas_call x1, Pallas kernels, sample(): pl.pallas_call(functools.partial(sample_kernel, cols, slabs, (rows_x, row...  8.41 us
    pallas_call x1, Pallas kernels, near(): pl.pallas_call(functools.partial(near_kernel, units, cols, slots, vecs),...  7.66 us
    all_to_all x2, waiting for transfers between devices, exchange(): lax.all_to_all(blocks, UNIT_AXES, split_axis=0, concat_axis=0, tiled=True)  3.69 us
    pallas_call x1, Pallas kernels, spectrum(): pl.pallas_call(functools.partial(spectrum_kernel, rows_x), out_shape=[plt...  3.66 us
    pallas_call x1, Pallas kernels, pack(): pl.pallas_call(functools.partial(pack_kernel, cols), out_shape=jax.ShapeD...  1.56 us
  transfers between devices with their start and end apart: 2, of which 1 were waited for; matrix products, arithmetic and copies ran while one was open for 0% of the time, Pallas kernels for 31%

profile of v3, /device:TPU:0, one launch (start us, length us, event | category | flops | bytes accessed | tf_op | source)
XLA Modules:
  0.0 36.7 jit_solution(17977159241784256904)
XLA Ops:
  0.0 1.6 %pack_inputs.1 = f32[16,16,128]{2,1,0:T(8,128)} custom-call(s32[1,1,2,2]{3,2,1,0:T(2,128)} %tiles_ref.1, f32[3,2,128]{2,1,0:T(2,128)} %noise_ref.1, s32[3,128]{1,0:T(4,128)} %offsets_ref.1, s32[1,1,16,16]{3,2,1,0:T(8,128)} %cells_ref.1, s32[1,128]{1,0:T(1,128)} %bitcast.1), custom_call_target="tpu_custom_call" | custom-call | tf_op jit(solution)/shard_map/pack_inputs/pallas_call | solution.py:161
  1.6 7.4 %all-to-all-start = ((f32[16,16,128]{2,1,0:T(8,128)}), f32[16,16,128]{2,1,0:T(8,128)S(1)}, u32[]{:S(2)}, u32[]{:S(2)}) async-start(f32[16,16,128]{2,1,0:T(8,128)} %pack_inputs.1), calls=%async_computation | async-start | bytes 262144 | tf_op jit(solution)/shard_map/all_to_all | solution.py:550
  9.0 3.7 %spectrum.1 = (bf16[768,2048]{1,0:T(8,128)(2,1)S(1)}, bf16[2,128,128]{2,1,0:T(8,128)(2,1)S(1)}) custom-call(f32[2,3,2,32,32,128]{5,4,3,2,1,0:T(8,128)} %spec_hbm.1, bf16[256,256]{1,0:T(8,128)(2,1)} %constant.10.clone.turn_hbm, f32[2,128,128]{2,1,0:T(8,128)} %constant.11.clone.wave_hbm), custom_call_target="tpu_custom_call" | custom-call | flops 805306368 | bytes 9437184 | tf_op jit(solution)/shard_map/spectrum/pallas_call | solution.py:257
  12.6 3.7 %all-to-all-done.packed_ref = f32[16,16,128]{2,1,0:T(8,128)S(1)} async-done(((f32[16,16,128]{2,1,0:T(8,128)}), f32[16,16,128]{2,1,0:T(8,128)S(1)}, u32[]{:S(2)}, u32[]{:S(2)}) %all-to-all-start) | async-done | bytes 131104 | tf_op jit(solution)/shard_map/all_to_all | solution.py:550
  16.3 8.4 %sample_far.1 = f32[16,3,2,128]{3,2,1,0:T(2,128)} custom-call(f32[16,16,128]{2,1,0:T(8,128)S(1)} %all-to-all-done.packed_ref, bf16[768,2048]{1,0:T(8,128)(2,1)S(1)} %get-tuple-element.7.field_ref, bf16[2,128,128]{2,1,0:T(8,128)(2,1)S(1)} %get-tuple-element.8.table_ref), custom_call_target="tpu_custom_call" | custom-call | flops 6442450944 | bytes 3145728 | tf_op jit(solution)/shard_map/sample_far/pallas_call | solution.py:382
  24.7 3.7 %all-to-all-start.1 = ((f32[16,3,2,128]{3,2,1,0:T(2,128)}), f32[16,3,2,128]{3,2,1,0:T(2,128)S(1)}, u32[]{:S(2)}, u32[]{:S(2)}) async-start(f32[16,3,2,128]{3,2,1,0:T(2,128)} %sample_far.1), calls=%async_computation.1 | async-start | bytes 98304 | tf_op jit(solution)/shard_map/all_to_all | solution.py:550
  28.4 7.7 %near_field.1 = f32[3,2,128]{2,1,0:T(2,128)S(1)} custom-call(f32[16,16,128]{2,1,0:T(8,128)S(1)} %all-to-all-done.packed_ref, bf16[2,3,2,64,896]{4,3,2,1,0:T(8,128)(2,1)} %constant.12.clone.table_hbm, bf16[2,3,2,64,896]{4,3,2,1,0:T(8,128)(2,1)} %constant.13.clone.energy_hbm), custom_call_target="tpu_custom_call" | custom-call | flops 4831838208 | bytes 8000000 | tf_op jit(solution)/shard_map/near_field/pallas_call | solution.py:529
  36.1 0.0 all-to-all-done.1
  36.1 0.6 %add.3 = f32[3,2,128]{2,1,0:T(2,128)} add(f32[3,2,128]{2,1,0:T(2,128)S(1)} %near_field.1, f32[3,2,128]{2,1,0:T(2,128)S(1)} %reduce_sum.9) | non-fusion elementwise | flops 768 | bytes 9216 | tf_op jit(solution)/shard_map/add | solution.py:559
  (1 shorter events, 0.0 us)
Async XLA Ops:
  1.6 14.7 %all-to-all-start = ((f32[16,16,128]{2,1,0:T(8,128)}), f32[16,16,128]{2,1,0:T(8,128)S(1)}, u32[]{:S(2)}, u32[]{:S(2)}) async-start(f32[16,16,128]{2,1,0:T(8,128)} %pack_inputs.1), calls=%async_computation | async-start | bytes 262144 | tf_op jit(solution)/shard_map/all_to_all | solution.py:550
  24.7 11.3 %all-to-all-start.1 = ((f32[16,3,2,128]{3,2,1,0:T(2,128)}), f32[16,3,2,128]{3,2,1,0:T(2,128)S(1)}, u32[]{:S(2)}, u32[]{:S(2)}) async-start(f32[16,3,2,128]{3,2,1,0:T(2,128)} %sample_far.1), calls=%async_computation.1 | async-start | bytes 98304 | tf_op jit(solution)/shard_map/all_to_all | solution.py:550

commit v4 on v3

--- a/solution.py
+++ b/solution.py
@@ -15,10 +15,12 @@
 SITES = PERIOD**3
 PLANE = PERIOD**2
 WINDOW = SITES + (PERIOD - 2) * PLANE
-OFFSETS, SLOT, ROW_TILE, COL_TILE, CELLS = 6, 9, 10, 11, 12
+HALVED = SITES // 2
+OFFSETS, SLOT, TILES, CELLS = 6, 9, 10, 11
+HALF = 256
 UNIT_AXES = ("row", "col")
 MIB = 1024 * 1024
-SPECTRUM_BYTES, SAMPLE_BYTES, NEAR_BYTES = 28 * MIB, 28 * MIB, 28 * MIB
+SPECTRUM_BYTES, SAMPLE_BYTES, NEAR_BYTES = 28 * MIB, 28 * MIB, 50 * MIB
 
 cheb_coef = (1.0, 0.45, -0.2, 0.12, -0.08)
 kernel_range = 1.5
@@ -31,9 +33,7 @@
     ids = np.arange(SITES)
     coords = np.stack([ids // PERIOD**2, ids // PERIOD % PERIOD, ids % PERIOD])
     half = PERIOD // 2
-    starts = np.stack([np.arange(WINDOW), np.arange(WINDOW) + PLANE])
-    columns = coords[:, starts % SITES]
-    displace = (coords[:, None, :PLANE, None] - columns[:, :, None, :] + half) % PERIOD - half
+    displace = (coords[:, :, None] - coords[:, None, :] + half) % PERIOD - half
     displace = displace.astype(np.float32)
     squares = (displace * displace).sum(0)
     scale_sq = np.float32(kernel_range * kernel_range)
@@ -47,9 +47,14 @@
     other = np.stack(other).astype(ml_dtypes.bfloat16)
     squared = [np.square(t.astype(np.float32)) for t in (same, other)]
     energy = squared[0] + squared[1] + np.roll(squared[1], 1, axis=0)
-    high = energy.astype(ml_dtypes.bfloat16)
-    low = (energy - high.astype(np.float32)).astype(ml_dtypes.bfloat16)
-    return np.stack([same, other]), np.stack([high, low])
+    columns = (np.arange(WINDOW)[None, :] + np.array([[0], [PLANE]])) % SITES
+    rows = np.stack([same, other])[:, :, :PLANE]
+    windows = np.stack([rows[..., shifted] for shifted in columns], axis=2)
+    first, last = energy[:, :HALVED, :HALVED], energy[:, :HALVED, HALVED:]
+    halves = 0.5 * np.stack([first + last, first - last], axis=1)
+    high = halves.astype(ml_dtypes.bfloat16)
+    low = (halves - high.astype(np.float32)).astype(ml_dtypes.bfloat16)
+    return windows, np.concatenate([high, low], axis=3)
 
 
 def whole_table(ref, kind, comp):
@@ -113,16 +118,15 @@
     slots = tiles_ref.shape[3]
     my_row, my_col = lax.axis_index("row"), lax.axis_index("col")
     lane = lax.broadcasted_iota(jnp.int32, (1, TB), 1)
-    row_tile = jnp.full((1, TB), -1, jnp.int32)
-    col_tile = jnp.full((1, TB), -1, jnp.int32)
+    tiles = jnp.full((1, TB), -1, jnp.int32)
     for slot in range(slots):
         tile_row = tiles_ref[0, 0, 0, slot]
         tile_col = tiles_ref[0, 0, 1, slot]
         active = tile_row >= 0
         row_unit = jnp.where(active, my_row * cols + tile_row, -1)
         col_unit = jnp.where(active, tile_col * cols + my_col, -1)
-        row_tile = jnp.where(lane == slot, row_unit, row_tile)
-        col_tile = jnp.where(lane == slot, col_unit, col_tile)
+        tiles = jnp.where(lane == slot, row_unit, tiles)
+        tiles = jnp.where(lane == slot + TB // 2, col_unit, tiles)
     cells = cells_ref[0, 0].astype(F32)
     caps, peers = cells.shape
     if peers < TB:
@@ -136,14 +140,16 @@
             ],
             axis=0,
         )
-    head = [offsets_ref[...], slot_ref[...], row_tile, col_tile]
+    cells = cells.astype(jnp.int32)
+    head = [offsets_ref[...], slot_ref[...], tiles]
+    head += [quotient(cells, 2 * HALF), remainder(cells, 2 * HALF) - HALF]
     block = jnp.concatenate(
-        [noise_ref[0], noise_ref[1], noise_ref[2]] + [part.astype(F32) for part in head] + [cells],
-        axis=0,
+        [noise_ref[0], noise_ref[1], noise_ref[2]] + [part.astype(F32) for part in head], axis=0
     )
     spare = out_ref.shape[1] - block.shape[0]
     if spare:
         block = jnp.concatenate([block, jnp.zeros((spare, TB), F32)], axis=0)
+    block = block.astype(BF16)
     for unit in range(units):
         out_ref[unit] = block
 
@@ -155,12 +161,12 @@
 
 def pack(noise_field, offsets, tile_list, send_cells, bead_slot, units, cols):
     _, lists = cell_rows(*send_cells.shape[2:])
-    rows = -(-(CELLS + lists) // 8) * 8
+    rows = -(-(CELLS + 2 * lists) // 16) * 16
     vmem = pl.BlockSpec(memory_space=pltpu.VMEM)
     smem = pl.BlockSpec(memory_space=pltpu.SMEM)
     return pl.pallas_call(
         functools.partial(pack_kernel, cols),
-        out_shape=jax.ShapeDtypeStruct((units, rows, TB), F32),
+        out_shape=jax.ShapeDtypeStruct((units, rows, TB), BF16),
         in_specs=[smem, vmem, vmem, vmem, vmem],
         out_specs=vmem,
         name="pack_inputs",
@@ -281,7 +287,10 @@
 def find_cells(cols, slabs, per_row, lists, packed_ref, first, group):
     units = packed_ref.shape[0]
     entries = units * lists
-    cells = packed_ref[:, CELLS : CELLS + lists, :].reshape(entries, TB).astype(jnp.int32)
+    packed = packed_ref[...].astype(F32)
+    high = packed[:, CELLS : CELLS + lists, :].reshape(entries, TB)
+    low = packed[:, CELLS + lists : CELLS + 2 * lists, :].reshape(entries, TB)
+    cells = (high * (2 * HALF) + (low + HALF)).astype(jnp.int32)
     entry = lax.broadcasted_iota(jnp.int32, cells.shape, 0)
     holder = quotient(entry, lists)
     holder_row = quotient(holder, cols)
@@ -295,7 +304,7 @@
     digits = jnp.concatenate([d.astype(F32).astype(BF16) for d in digits], axis=1)
     beads = group * TB
     slot = jnp.concatenate(
-        [packed_ref[first + unit, SLOT : SLOT + 1, :] for unit in range(group)], axis=1
+        [packed_ref[first + unit].astype(F32)[SLOT : SLOT + 1] for unit in range(group)], axis=1
     ).astype(jnp.int32)
     owner = first + quotient(lax.broadcasted_iota(jnp.int32, (1, beads), 1), TB)
     order = quotient(slot, units)
@@ -383,7 +392,7 @@
         functools.partial(sample_kernel, cols, slabs, (rows_x, rows_y), lists, groups),
         grid=(units // whole,),
         out_shape=jax.ShapeDtypeStruct((units, comps, vecs, TB), F32),
-        in_specs=[vmem, vmem, vmem],
+        in_specs=[vmem] * 3,
         out_specs=pl.BlockSpec((whole, comps, vecs, TB), lambda i: (i, 0, 0, 0)),
         scratch_shapes=[pltpu.VMEM((2 * depth, group * TB), BF16) for group in groups],
         compiler_params=pltpu.CompilerParams(vmem_limit_bytes=SAMPLE_BYTES),
@@ -396,9 +405,23 @@
     )(packed, field, table)
 
 
+def over(count, term, sum_refs):
+    if not sum_refs:
+        return functools.reduce(lambda a, b: a + b, [term(at) for at in range(count)])
+    sum_ref = sum_refs[0]
+    sum_ref[...] = term(0)
+
+    def step(at, carry):
+        sum_ref[...] += term(at)
+        return carry
+
+    lax.fori_loop(1, count, step, 0)
+    return sum_ref[...]
+
+
 def near_kernel(
-    units, cols, slots, vecs, packed_ref, table_hbm, energy_hbm, out_ref,
-    table_ref, energy_ref, rows_ref, sems,
+    units, cols, slots, vecs, packed_ref, noise_ref, table_hbm, energy_hbm, out_ref,
+    table_ref, energy_ref, rows_ref, sems, *sum_refs,
 ):
     copies = [
         pltpu.make_async_copy(table_hbm, table_ref, sems.at[0]),
@@ -406,6 +429,7 @@
     ]
     for copy in copies:
         copy.start()
+
     part = vecs * units
     wide = 4 * part
     fields = 3 * vecs
@@ -414,36 +438,37 @@
     block_of = quotient(lax.broadcasted_iota(jnp.int32, (SITES, wide), 1), part)
 
     def sites_of(unit):
-        rows = [packed_ref[unit, OFFSETS + axis : OFFSETS + axis + 1, :] for axis in range(3)]
-        code = (rows[0] * PERIOD + rows[1]) * PERIOD + rows[2]
+        rows = packed_ref[unit].astype(F32)[OFFSETS : OFFSETS + 3]
+        code = (rows[0:1] * PERIOD + rows[1:2]) * PERIOD + rows[2:3]
         return jnp.where(site == code.astype(jnp.int32), 1.0, 0.0).astype(BF16)
 
-    lattice = None
-    for first in range(0, units, group):
+    def scatter(first):
         held, spread = [], []
-        for unit in range(first, first + group):
+        for at in range(group):
+            unit = first + at
             held.append(sites_of(unit))
-            high, low = split(packed_ref[unit, 0:fields, :])
-            ones, zeros = jnp.ones((vecs, TB), F32), jnp.zeros((vecs, TB), F32)
-            pieces = jnp.concatenate([high.astype(F32), ones, low.astype(F32), zeros], axis=0)
-            mine = lax.broadcasted_iota(jnp.int32, (8 * vecs, units, TB), 1) == unit
+            noise = packed_ref[unit].astype(F32)[0:fields]
+            pieces = jnp.concatenate([noise, jnp.ones((vecs, TB), F32)], axis=0)
+            mine = lax.broadcasted_iota(jnp.int32, (4 * vecs, units, TB), 1) == unit
             block = jnp.where(mine, pieces[:, None, :], 0.0)
-            spread.append(block.reshape(2 * wide, TB).astype(BF16))
-        term = dot_nt(jnp.concatenate(held, axis=1), jnp.concatenate(spread, axis=1))
-        lattice = term if lattice is None else lattice + term
-    lattice = lattice[:, :wide] + lattice[:, wide:]
+            spread.append(block.reshape(wide, TB).astype(BF16))
+        return dot_nt(jnp.concatenate(held, axis=1), jnp.concatenate(spread, axis=1))
+
+    lattice = over(units // group, lambda at: scatter(at * group), sum_refs[:1])
     to_all = lax.broadcasted_iota(jnp.int32, (wide, wide), 0) == 3 * part + remainder(
         lax.broadcasted_iota(jnp.int32, (wide, wide), 1), units
     )
     count = dot(lattice.astype(BF16), jnp.where(to_all, 1.0, 0.0).astype(BF16))
 
     lane = lax.broadcasted_iota(jnp.int32, (units, wide), 1)
-    row_tiles = packed_ref[:, ROW_TILE, :].astype(jnp.int32)
-    col_tiles = packed_ref[:, COL_TILE, :].astype(jnp.int32)
-    mix = None
-    for slot in range(slots):
-        row_unit = row_tiles[:, slot : slot + 1]
-        col_unit = col_tiles[:, slot : slot + 1]
+    tiles = packed_ref[...].astype(F32)[:, TILES, :].astype(jnp.int32)
+    tile_lane = lax.broadcasted_iota(jnp.int32, (units, TB), 1)
+
+    def links(slot):
+        row_unit, col_unit = [
+            jnp.sum(jnp.where(tile_lane == slot + start, tiles, 0), axis=1, keepdims=True)
+            for start in (0, TB // 2)
+        ]
         active = row_unit >= 0
         from_col, to_row = [], []
         for vec in range(vecs):
@@ -458,8 +483,9 @@
                     jnp.concatenate([hot(row_unit, (comp - turn) % 3) for turn in range(3)], axis=1)
                 )
         from_col = jnp.concatenate(from_col, axis=0).astype(BF16)
-        term = dot_tn(from_col, jnp.concatenate(to_row, axis=0).astype(BF16))
-        mix = term if mix is None else mix + term
+        return dot_tn(from_col, jnp.concatenate(to_row, axis=0).astype(BF16))
+
+    mix = over(slots, links, sum_refs[1:])
     mix = mix.astype(BF16)
     mix = jnp.concatenate([mix, mix], axis=0)
 
@@ -469,11 +495,13 @@
     for copy in copies:
         copy.wait()
 
-    exact = count.astype(BF16)
-    energy = sum(
-        in_block(comp, sum(dot(whole_table(energy_ref, kind, comp), exact) for kind in range(2)))
-        for comp in range(3)
-    )
+    halves = (count[:HALVED] + count[HALVED:], count[:HALVED] - count[HALVED:])
+    halves = [jnp.concatenate([half.astype(BF16)] * 2, axis=0) for half in halves]
+    energy = None
+    for comp in range(3):
+        plus, minus = [dot(energy_ref[comp, kind], half) for kind, half in enumerate(halves)]
+        term = in_block(comp, jnp.concatenate([plus + minus, plus - minus], axis=0))
+        energy = term if energy is None else energy + term
     energy = dot(jnp.concatenate(split(energy), axis=1), mix[:, :wide])
     occupied = (count > 0.5) & (block_of < 3)
     largest = jnp.max(jnp.where(occupied, energy, 0.0), keepdims=True)
@@ -517,34 +545,35 @@
     for comp in range(3):
         for vec in range(vecs):
             near = rows_ref[pl.ds(comp * part + vec * units + me, 1), :] * scaling
-            at = comp * vecs + vec
-            noise = packed_ref[me, at : at + 1, :]
-            out_ref[comp, vec : vec + 1, :] = first_weight * noise + near
-
-
-def near(packed, units, cols, slots, vecs):
+            out_ref[comp, vec : vec + 1, :] = first_weight * noise_ref[comp, vec : vec + 1, :] + near
+
+
+def near(packed, noise_field, units, cols, slots):
+    vecs = noise_field.shape[1]
+    wide = 4 * vecs * units
     tables = kernel_tables()
     vmem = pl.BlockSpec(memory_space=pltpu.VMEM)
     hbm = pl.BlockSpec(memory_space=pltpu.HBM)
+    sums = [(SITES, wide), (wide, 3 * wide)] if units > 16 else []
     return pl.pallas_call(
         functools.partial(near_kernel, units, cols, slots, vecs),
         out_shape=pltpu.VMEM((3, vecs, TB), F32),
-        in_specs=[vmem] + [hbm] * 2,
+        in_specs=[vmem] * 2 + [hbm] * 2,
         out_specs=vmem,
         scratch_shapes=[pltpu.VMEM(table.shape, BF16) for table in tables]
-        + [pltpu.VMEM((4 * vecs * units, TB), F32), pltpu.SemaphoreType.DMA((2,))],
+        + [pltpu.VMEM((wide, TB), F32), pltpu.SemaphoreType.DMA((2,))]
+        + [pltpu.VMEM(shape, F32) for shape in sums],
         compiler_params=pltpu.CompilerParams(vmem_limit_bytes=NEAR_BYTES),
         cost_estimate=pl.CostEstimate(
             flops=4 * 2 * 9 * SITES * SITES * 256, bytes_accessed=8 * 10**6, transcendentals=0
         ),
         name="near_field",
-    )(packed, *in_hbm(tables))
+    )(packed, noise_field, *in_hbm(tables))
 
 
 def per_device(noise_field, offsets, tile_list, send_cells, bead_slot, spectral):
     rows, cols = lax.axis_size("row"), lax.axis_size("col")
     units = rows * cols
-    vecs = noise_field.shape[1]
 
     def exchange(blocks):
         return lax.all_to_all(blocks, UNIT_AXES, split_axis=0, concat_axis=0, tiled=True)
@@ -555,7 +584,7 @@
     field, waves = spectrum(spectral)
     far = sample(packed, field, waves, spectral.shape, send_cells.shape, rows, cols)
     partial = exchange(far)
-    near_field = near(packed, units, cols, tile_list.shape[3], vecs)
+    near_field = near(packed, noise_field, units, cols, tile_list.shape[3])
     return near_field + jnp.sum(partial, axis=0)
 
 

time: 37 us -> 36.1 us (0.976)
  waiting for transfers between devices: 3.69 us -> 2.97 us
    all_to_all x2, waiting for transfers between devices: 3.69 us -> 2.97 us  [exchange(): lax.all_to_all(blocks, UNIT_AXES, split_axis=0, concat_axis=0, tiled=True)]
where the time goes in v4:
time: 36.1 us; the launch traced here: 35.8 us
  Pallas kernels  21.1 us (58%)
  starting transfers between devices  11.1 us (31%)
  waiting for transfers between devices  2.97 us (8%)
  other arithmetic  0.62 us (2%)
    all_to_all x2, starting transfers between devices, exchange(): lax.all_to_all(blocks, UNIT_AXES, split_axis=0, concat_axis=0, tiled=True)  11.1 us
    pallas_call x1, Pallas kernels, sample(): pl.pallas_call(functools.partial(sample_kernel, cols, slabs, (rows_x, row...  8.52 us
    pallas_call x1, Pallas kernels, near(): pl.pallas_call(functools.partial(near_kernel, units, cols, slots, vecs),...  7.35 us
    pallas_call x1, Pallas kernels, spectrum(): pl.pallas_call(functools.partial(spectrum_kernel, rows_x), out_shape=[plt...  3.66 us
    all_to_all x2, waiting for transfers between devices, exchange(): lax.all_to_all(blocks, UNIT_AXES, split_axis=0, concat_axis=0, tiled=True)  2.97 us
    pallas_call x1, Pallas kernels, pack(): pl.pallas_call(functools.partial(pack_kernel, cols), out_shape=jax.ShapeD...  1.53 us
  transfers between devices with their start and end apart: 2, of which 1 were waited for; matrix products, arithmetic and copies ran while one was open for 0% of the time, Pallas kernels for 31%

profile of v4, /device:TPU:0, one launch (start us, length us, event | category | flops | bytes accessed | tf_op | source)
XLA Modules:
  0.0 35.8 jit_solution(16802636060695129362)
XLA Ops:
  0.0 1.5 %pack_inputs.1 = bf16[16,16,128]{2,1,0:T(8,128)(2,1)} custom-call(s32[1,1,2,2]{3,2,1,0:T(2,128)} %tiles_ref.1, f32[3,2,128]{2,1,0:T(2,128)} %noise_ref.3, s32[3,128]{1,0:T(4,128)} %offsets_ref.1, s32[1,1,16,16]{3,2,1,0:T(8,128)} %cells_ref.1, s32[1,128]{1,0:T(1,128)} %bitcast.1), custom_call_target="tpu_custom_call" | custom-call | tf_op jit(solution)/shard_map/pack_inputs/pallas_call | solution.py:167
  1.5 7.4 %all-to-all-start = ((bf16[16,16,128]{2,1,0:T(8,128)(2,1)}), bf16[16,16,128]{2,1,0:T(8,128)(2,1)S(1)}, u32[]{:S(2)}, u32[]{:S(2)}) async-start(bf16[16,16,128]{2,1,0:T(8,128)(2,1)} %pack_inputs.1), calls=%async_computation | async-start | bytes 131072 | tf_op jit(solution)/shard_map/all_to_all | solution.py:579
  8.9 3.7 %spectrum.1 = (bf16[768,2048]{1,0:T(8,128)(2,1)S(1)}, bf16[2,128,128]{2,1,0:T(8,128)(2,1)S(1)}) custom-call(f32[2,3,2,32,32,128]{5,4,3,2,1,0:T(8,128)} %spec_hbm.1, bf16[256,256]{1,0:T(8,128)(2,1)} %constant.10.clone.turn_hbm, f32[2,128,128]{2,1,0:T(8,128)} %constant.11.clone.wave_hbm), custom_call_target="tpu_custom_call" | custom-call | flops 805306368 | bytes 9437184 | tf_op jit(solution)/shard_map/spectrum/pallas_call | solution.py:263
  12.6 3.0 %all-to-all-done.packed_ref = bf16[16,16,128]{2,1,0:T(8,128)(2,1)S(1)} async-done(((bf16[16,16,128]{2,1,0:T(8,128)(2,1)}), bf16[16,16,128]{2,1,0:T(8,128)(2,1)S(1)}, u32[]{:S(2)}, u32[]{:S(2)}) %all-to-all-start) | async-done | bytes 65568 | tf_op jit(solution)/shard_map/all_to_all | solution.py:579
  15.6 0.0 copy-start
  15.6 8.5 %sample_far.1 = f32[16,3,2,128]{3,2,1,0:T(2,128)} custom-call(bf16[16,16,128]{2,1,0:T(8,128)(2,1)S(1)} %all-to-all-done.packed_ref, bf16[768,2048]{1,0:T(8,128)(2,1)S(1)} %get-tuple-element.7.field_ref, bf16[2,128,128]{2,1,0:T(8,128)(2,1)S(1)} %get-tuple-element.8.table_ref), custom_call_target="tpu_custom_call" | custom-call | flops 6442450944 | bytes 3145728 | tf_op jit(solution)/shard_map/sample_far/pallas_call | solution.py:391
  24.1 3.7 %all-to-all-start.1 = ((f32[16,3,2,128]{3,2,1,0:T(2,128)}), f32[16,3,2,128]{3,2,1,0:T(2,128)S(1)}, u32[]{:S(2)}, u32[]{:S(2)}) async-start(f32[16,3,2,128]{3,2,1,0:T(2,128)} %sample_far.1), calls=%async_computation.1 | async-start | bytes 98304 | tf_op jit(solution)/shard_map/all_to_all | solution.py:579
  27.8 0.0 copy-done
  27.8 7.4 %near_field.1 = f32[3,2,128]{2,1,0:T(2,128)S(1)} custom-call(bf16[16,16,128]{2,1,0:T(8,128)(2,1)S(1)} %all-to-all-done.packed_ref, f32[3,2,128]{2,1,0:T(2,128)S(1)} %copy-done, bf16[2,3,2,64,896]{4,3,2,1,0:T(8,128)(2,1)} %constant.12.clone.table_hbm, bf16[3,2,256,512]{3,2,1,0:T(8,128)(2,1)} %constant.13.clone.energy_hbm), custom_call_target="tpu_custom_call" | custom-call | flops 4831838208 | bytes 8000000 | tf_op jit(solution)/shard_map/near_field/pallas_call | solution.py:558
  35.1 0.0 all-to-all-done.1
  35.2 0.6 %add.3 = f32[3,2,128]{2,1,0:T(2,128)} add(f32[3,2,128]{2,1,0:T(2,128)S(1)} %near_field.1, f32[3,2,128]{2,1,0:T(2,128)S(1)} %reduce_sum.9) | non-fusion elementwise | flops 768 | bytes 9216 | tf_op jit(solution)/shard_map/add | solution.py:588
  (1 shorter events, 0.0 us)
Async XLA Ops:
  1.5 14.0 %all-to-all-start = ((bf16[16,16,128]{2,1,0:T(8,128)(2,1)}), bf16[16,16,128]{2,1,0:T(8,128)(2,1)S(1)}, u32[]{:S(2)}, u32[]{:S(2)}) async-start(bf16[16,16,128]{2,1,0:T(8,128)(2,1)} %pack_inputs.1), calls=%async_computation | async-start | bytes 131072 | tf_op jit(solution)/shard_map/all_to_all | solution.py:579
  15.6 12.2 %copy-start = (f32[3,2,128]{2,1,0:T(2,128)S(1)}, f32[3,2,128]{2,1,0:T(2,128)}, u32[]{:S(2)}) copy-start(f32[3,2,128]{2,1,0:T(2,128)} %noise_ref.3) | copy-start | bytes 9220
  24.1 11.1 %all-to-all-start.1 = ((f32[16,3,2,128]{3,2,1,0:T(2,128)}), f32[16,3,2,128]{3,2,1,0:T(2,128)S(1)}, u32[]{:S(2)}, u32[]{:S(2)}) async-start(f32[16,3,2,128]{3,2,1,0:T(2,128)} %sample_far.1), calls=%async_computation.1 | async-start | bytes 98304 | tf_op jit(solution)/shard_map/all_to_all | solution.py:579

commit v5 on v4

--- a/solution.py
+++ b/solution.py
@@ -50,11 +50,25 @@
     columns = (np.arange(WINDOW)[None, :] + np.array([[0], [PLANE]])) % SITES
     rows = np.stack([same, other])[:, :, :PLANE]
     windows = np.stack([rows[..., shifted] for shifted in columns], axis=2)
-    first, last = energy[:, :HALVED, :HALVED], energy[:, :HALVED, HALVED:]
-    halves = 0.5 * np.stack([first + last, first - last], axis=1)
+    energy_halves = halved_tables(energy)
+    pair_halves = halved_tables(np.stack([same, other]).astype(np.float32))[0]
+    pair_halves = np.moveaxis(pair_halves, 2, 1).reshape(2, 2, 3 * HALVED, HALVED)
+    return windows, np.concatenate(energy_halves, axis=3), pair_halves
+
+
+def halved_tables(tables):
+    first, last = tables[..., :HALVED, :HALVED], tables[..., :HALVED, HALVED:]
+    halves = 0.5 * np.stack([first + last, first - last], axis=-3)
     high = halves.astype(ml_dtypes.bfloat16)
-    low = (halves - high.astype(np.float32)).astype(ml_dtypes.bfloat16)
-    return windows, np.concatenate([high, low], axis=3)
+    return high, (halves - high.astype(np.float32)).astype(ml_dtypes.bfloat16)
+
+
+def halve(value):
+    return value[:HALVED] + value[HALVED:], value[:HALVED] - value[HALVED:]
+
+
+def unhalve(plus, minus):
+    return jnp.concatenate([plus + minus, plus - minus], axis=0)
 
 
 def whole_table(ref, kind, comp):
@@ -120,8 +134,8 @@
     lane = lax.broadcasted_iota(jnp.int32, (1, TB), 1)
     tiles = jnp.full((1, TB), -1, jnp.int32)
     for slot in range(slots):
-        tile_row = tiles_ref[0, 0, 0, slot]
-        tile_col = tiles_ref[0, 0, 1, slot]
+        tile_row = tiles_ref[0, 0, 0:1, slot : slot + 1]
+        tile_col = tiles_ref[0, 0, 1:2, slot : slot + 1]
         active = tile_row >= 0
         row_unit = jnp.where(active, my_row * cols + tile_row, -1)
         col_unit = jnp.where(active, tile_col * cols + my_col, -1)
@@ -163,11 +177,10 @@
     _, lists = cell_rows(*send_cells.shape[2:])
     rows = -(-(CELLS + 2 * lists) // 16) * 16
     vmem = pl.BlockSpec(memory_space=pltpu.VMEM)
-    smem = pl.BlockSpec(memory_space=pltpu.SMEM)
     return pl.pallas_call(
         functools.partial(pack_kernel, cols),
         out_shape=jax.ShapeDtypeStruct((units, rows, TB), BF16),
-        in_specs=[smem, vmem, vmem, vmem, vmem],
+        in_specs=[vmem] * 5,
         out_specs=vmem,
         name="pack_inputs",
     )(tile_list, noise_field, offsets, send_cells, bead_slot.reshape(1, TB))
@@ -420,12 +433,13 @@
 
 
 def near_kernel(
-    units, cols, slots, vecs, packed_ref, noise_ref, table_hbm, energy_hbm, out_ref,
-    table_ref, energy_ref, rows_ref, sems, *sum_refs,
+    units, cols, slots, vecs, packed_ref, noise_ref, table_hbm, energy_hbm, half_hbm, out_ref,
+    table_ref, energy_ref, half_ref, rows_ref, sems, *sum_refs,
 ):
     copies = [
         pltpu.make_async_copy(table_hbm, table_ref, sems.at[0]),
         pltpu.make_async_copy(energy_hbm, energy_ref, sems.at[1]),
+        pltpu.make_async_copy(half_hbm, half_ref, sems.at[2]),
     ]
     for copy in copies:
         copy.start()
@@ -492,15 +506,17 @@
     def in_block(block, value):
         return jnp.where(block_of == block, value, 0.0)
 
-    for copy in copies:
+    def in_half_block(block, value):
+        return jnp.where(block_of[:HALVED] == block, value, 0.0)
+
+    for copy in copies[:2]:
         copy.wait()
 
-    halves = (count[:HALVED] + count[HALVED:], count[:HALVED] - count[HALVED:])
-    halves = [jnp.concatenate([half.astype(BF16)] * 2, axis=0) for half in halves]
+    halves = [jnp.concatenate([half.astype(BF16)] * 2, axis=0) for half in halve(count)]
     energy = None
     for comp in range(3):
         plus, minus = [dot(energy_ref[comp, kind], half) for kind, half in enumerate(halves)]
-        term = in_block(comp, jnp.concatenate([plus + minus, plus - minus], axis=0))
+        term = in_block(comp, unhalve(plus, minus))
         energy = term if energy is None else energy + term
     energy = dot(jnp.concatenate(split(energy), axis=1), mix[:, :wide])
     occupied = (count > 0.5) & (block_of < 3)
@@ -519,6 +535,22 @@
             result = term if result is None else result + term
         return result
 
+    def halved_product(vector):
+        mixed = dot(jnp.concatenate(split(jnp.concatenate(halve(vector), axis=0)), axis=1), mix).astype(BF16)
+        results = []
+        for kind in range(2):
+            half = mixed[kind * HALVED : (kind + 1) * HALVED]
+            same = dot(half_ref[0, kind], half[:, :wide])
+            other = dot(half_ref[1, kind], half[:, wide:])
+            result = None
+            for comp in range(3):
+                rows = slice(comp * HALVED, (comp + 1) * HALVED)
+                term = in_half_block(comp, same[rows] + other[rows, :wide])
+                term = term + in_half_block((comp + 1) % 3, other[rows, wide:])
+                result = term if result is None else result + term
+            results.append(result)
+        return unhalve(*results)
+
     weights = (
         cheb_coef[1] - cheb_coef[3],
         2.0 * (cheb_coef[2] - cheb_coef[4]),
@@ -528,7 +560,9 @@
     weight = count * scaling
     previous, current, total = None, lattice, None
     for degree in range(4):
-        result = product(current)
+        if degree == 1:
+            copies[2].wait()
+        result = product(current) if degree < 1 else halved_product(current)
         scaled = weights[degree] * result
         total = scaled if total is None else total + scaled
         if degree < 3:
@@ -558,10 +592,10 @@
     return pl.pallas_call(
         functools.partial(near_kernel, units, cols, slots, vecs),
         out_shape=pltpu.VMEM((3, vecs, TB), F32),
-        in_specs=[vmem] * 2 + [hbm] * 2,
+        in_specs=[vmem] * 2 + [hbm] * 3,
         out_specs=vmem,
         scratch_shapes=[pltpu.VMEM(table.shape, BF16) for table in tables]
-        + [pltpu.VMEM((wide, TB), F32), pltpu.SemaphoreType.DMA((2,))]
+        + [pltpu.VMEM((wide, TB), F32), pltpu.SemaphoreType.DMA((3,))]
         + [pltpu.VMEM(shape, F32) for shape in sums],
         compiler_params=pltpu.CompilerParams(vmem_limit_bytes=NEAR_BYTES),
         cost_estimate=pl.CostEstimate(

time: 36.1 us -> 35.1 us (0.972)
  Pallas kernels: 21.1 us -> 20.1 us
    pallas_call x1, Pallas kernels: 7.35 us -> 6.51 us  [near(): pl.pallas_call(functools.partial(near_kernel, units, cols, slots, vecs),...]
  transfers between devices with their start and end apart: 2 -> 2, of which waited for: 1 -> 1; matrix products, arithmetic and copies ran while one was open for 0% -> 0% of each run, Pallas kernels for 31% -> 29%
where the time goes in v5:
time: 35.1 us; the launch traced here: 34.8 us
  Pallas kernels  20.1 us (57%)
  starting transfers between devices  11.1 us (32%)
  waiting for transfers between devices  2.97 us (8%)
  other arithmetic  0.62 us (2%)
    all_to_all x2, starting transfers between devices, exchange(): lax.all_to_all(blocks, UNIT_AXES, split_axis=0, concat_axis=0, tiled=True)  11.1 us
    pallas_call x1, Pallas kernels, sample(): pl.pallas_call(functools.partial(sample_kernel, cols, slabs, (rows_x, row...  8.52 us
    pallas_call x1, Pallas kernels, near(): pl.pallas_call(functools.partial(near_kernel, units, cols, slots, vecs),...  6.51 us
    pallas_call x1, Pallas kernels, spectrum(): pl.pallas_call(functools.partial(spectrum_kernel, rows_x), out_shape=[plt...  3.66 us
    all_to_all x2, waiting for transfers between devices, exchange(): lax.all_to_all(blocks, UNIT_AXES, split_axis=0, concat_axis=0, tiled=True)  2.97 us
    pallas_call x1, Pallas kernels, pack(): pl.pallas_call(functools.partial(pack_kernel, cols), out_shape=jax.ShapeD...  1.44 us
  transfers between devices with their start and end apart: 2, of which 1 were waited for; matrix products, arithmetic and copies ran while one was open for 0% of the time, Pallas kernels for 29%

profile of v5, /device:TPU:0, one launch (start us, length us, event | category | flops | bytes accessed | tf_op | source)
XLA Modules:
  0.0 34.8 jit_solution(13284925515042112729)
XLA Ops:
  0.0 1.4 %pack_inputs.1 = bf16[16,16,128]{2,1,0:T(8,128)(2,1)} custom-call(s32[1,1,2,2]{3,2,1,0:T(2,128)} %tiles_ref.1, f32[3,2,128]{2,1,0:T(2,128)} %noise_ref.3, s32[3,128]{1,0:T(4,128)} %offsets_ref.1, s32[1,1,16,16]{3,2,1,0:T(8,128)} %cells_ref.1, s32[1,128]{1,0:T(1,128)} %bitcast.1), custom_call_target="tpu_custom_call" | custom-call | tf_op jit(solution)/shard_map/pack_inputs/pallas_call | solution.py:180
  1.4 7.4 %all-to-all-start = ((bf16[16,16,128]{2,1,0:T(8,128)(2,1)}), bf16[16,16,128]{2,1,0:T(8,128)(2,1)S(1)}, u32[]{:S(2)}, u32[]{:S(2)}) async-start(bf16[16,16,128]{2,1,0:T(8,128)(2,1)} %pack_inputs.1), calls=%async_computation | async-start | bytes 131072 | tf_op jit(solution)/shard_map/all_to_all | solution.py:613
  8.8 3.7 %spectrum.1 = (bf16[768,2048]{1,0:T(8,128)(2,1)S(1)}, bf16[2,128,128]{2,1,0:T(8,128)(2,1)S(1)}) custom-call(f32[2,3,2,32,32,128]{5,4,3,2,1,0:T(8,128)} %spec_hbm.1, bf16[256,256]{1,0:T(8,128)(2,1)} %constant.12.clone.turn_hbm, f32[2,128,128]{2,1,0:T(8,128)} %constant.13.clone.wave_hbm), custom_call_target="tpu_custom_call" | custom-call | flops 805306368 | bytes 9437184 | tf_op jit(solution)/shard_map/spectrum/pallas_call | solution.py:276
  12.5 3.0 %all-to-all-done.packed_ref = bf16[16,16,128]{2,1,0:T(8,128)(2,1)S(1)} async-done(((bf16[16,16,128]{2,1,0:T(8,128)(2,1)}), bf16[16,16,128]{2,1,0:T(8,128)(2,1)S(1)}, u32[]{:S(2)}, u32[]{:S(2)}) %all-to-all-start) | async-done | bytes 65568 | tf_op jit(solution)/shard_map/all_to_all | solution.py:613
  15.5 0.0 copy-start
  15.5 8.5 %sample_far.1 = f32[16,3,2,128]{3,2,1,0:T(2,128)} custom-call(bf16[16,16,128]{2,1,0:T(8,128)(2,1)S(1)} %all-to-all-done.packed_ref, bf16[768,2048]{1,0:T(8,128)(2,1)S(1)} %get-tuple-element.7.field_ref, bf16[2,128,128]{2,1,0:T(8,128)(2,1)S(1)} %get-tuple-element.8.table_ref), custom_call_target="tpu_custom_call" | custom-call | flops 6442450944 | bytes 3145728 | tf_op jit(solution)/shard_map/sample_far/pallas_call | solution.py:404
  24.0 3.7 %all-to-all-start.1 = ((f32[16,3,2,128]{3,2,1,0:T(2,128)}), f32[16,3,2,128]{3,2,1,0:T(2,128)S(1)}, u32[]{:S(2)}, u32[]{:S(2)}) async-start(f32[16,3,2,128]{3,2,1,0:T(2,128)} %sample_far.1), calls=%async_computation.1 | async-start | bytes 98304 | tf_op jit(solution)/shard_map/all_to_all | solution.py:613
  27.7 0.0 copy-done
  27.7 6.5 %near_field.1 = f32[3,2,128]{2,1,0:T(2,128)S(1)} custom-call(bf16[16,16,128]{2,1,0:T(8,128)(2,1)S(1)} %all-to-all-done.packed_ref, f32[3,2,128]{2,1,0:T(2,128)S(1)} %copy-done, bf16[2,3,2,64,896]{4,3,2,1,0:T(8,128)(2,1)} %constant.14.clone.table_hbm, bf16[3,2,256,512]{3,2,1,0:T(8,128)(2,1)} %constant.15.clone.energy_hbm, ...), custom_call_target="tpu_custom_call" | custom-call | flops 4831838208 | bytes 8000000 | tf_op jit(solution)/shard_map/near_field/pallas_call | solution.py:592
  34.2 0.0 all-to-all-done.1
  34.2 0.6 %add.3 = f32[3,2,128]{2,1,0:T(2,128)} add(f32[3,2,128]{2,1,0:T(2,128)S(1)} %near_field.1, f32[3,2,128]{2,1,0:T(2,128)S(1)} %reduce_sum.9) | non-fusion elementwise | flops 768 | bytes 9216 | tf_op jit(solution)/shard_map/add | solution.py:622
  (1 shorter events, 0.0 us)
Async XLA Ops:
  1.4 14.0 %all-to-all-start = ((bf16[16,16,128]{2,1,0:T(8,128)(2,1)}), bf16[16,16,128]{2,1,0:T(8,128)(2,1)S(1)}, u32[]{:S(2)}, u32[]{:S(2)}) async-start(bf16[16,16,128]{2,1,0:T(8,128)(2,1)} %pack_inputs.1), calls=%async_computation | async-start | bytes 131072 | tf_op jit(solution)/shard_map/all_to_all | solution.py:613
  15.5 12.2 %copy-start = (f32[3,2,128]{2,1,0:T(2,128)S(1)}, f32[3,2,128]{2,1,0:T(2,128)}, u32[]{:S(2)}) copy-start(f32[3,2,128]{2,1,0:T(2,128)} %noise_ref.3) | copy-start | bytes 9220
  24.0 10.2 %all-to-all-start.1 = ((f32[16,3,2,128]{3,2,1,0:T(2,128)}), f32[16,3,2,128]{3,2,1,0:T(2,128)S(1)}, u32[]{:S(2)}, u32[]{:S(2)}) async-start(f32[16,3,2,128]{3,2,1,0:T(2,128)} %sample_far.1), calls=%async_computation.1 | async-start | bytes 98304 | tf_op jit(solution)/shard_map/all_to_all | solution.py:613

commit v6 on v5

--- a/solution.py
+++ b/solution.py
@@ -368,6 +368,11 @@
             phase_ref[at : at + rows_y, :] = cos_one * sin_y + sin_one * cos_y
         return place[2]
 
+    def order(unit):
+        if out_ref.shape[0] != packed_ref.shape[0]:
+            return unit
+        return unit % cols * (packed_ref.shape[0] // cols) + unit // cols
+
     def finish(first, group, total, place_z):
         chosen = hits(place_z)
         for comp in range(comps):
@@ -376,7 +381,8 @@
                 picked = jnp.where(chosen, total[at : at + length], 0.0)
                 picked = jnp.sum(picked, axis=0, keepdims=True)
                 for unit in range(group):
-                    out_ref[first + unit, comp, vec : vec + 1, :] = picked[
+                    owner = order(first + unit)
+                    out_ref[owner, comp, vec : vec + 1, :] = picked[
                         :, unit * TB : (unit + 1) * TB
                     ]
 
@@ -609,15 +615,15 @@
     rows, cols = lax.axis_size("row"), lax.axis_size("col")
     units = rows * cols
 
-    def exchange(blocks):
-        return lax.all_to_all(blocks, UNIT_AXES, split_axis=0, concat_axis=0, tiled=True)
+    def exchange(blocks, axes=UNIT_AXES):
+        return lax.all_to_all(blocks, axes, split_axis=0, concat_axis=0, tiled=True)
 
     packed = exchange(
         pack(noise_field, offsets, tile_list, send_cells, bead_slot, units, cols)
     )
     field, waves = spectrum(spectral)
     far = sample(packed, field, waves, spectral.shape, send_cells.shape, rows, cols)
-    partial = exchange(far)
+    partial = exchange(far, UNIT_AXES[::-1] if units == 16 else UNIT_AXES)
     near_field = near(packed, noise_field, units, cols, tile_list.shape[3])
     return near_field + jnp.sum(partial, axis=0)
 

time: 35.1 us -> 35.1 us (level)
  no operation moved by 1% of the time
where the time goes in v6:
time: 35.1 us; the launch traced here: 34.8 us
  Pallas kernels  20.1 us (57%)
  starting transfers between devices  11.1 us (32%)
  waiting for transfers between devices  2.98 us (8%)
  other arithmetic  0.62 us (2%)
    all_to_all x2, starting transfers between devices, exchange(): return lax.all_to_all(blocks, axes, split_axis=0, concat_axis=0, tiled=True)  11.1 us
    pallas_call x1, Pallas kernels, sample(): pl.pallas_call(functools.partial(sample_kernel, cols, slabs, (rows_x, row...  8.52 us
    pallas_call x1, Pallas kernels, near(): pl.pallas_call(functools.partial(near_kernel, units, cols, slots, vecs),...  6.51 us
    pallas_call x1, Pallas kernels, spectrum(): pl.pallas_call(functools.partial(spectrum_kernel, rows_x), out_shape=[plt...  3.66 us
    all_to_all x2, waiting for transfers between devices, exchange(): return lax.all_to_all(blocks, axes, split_axis=0, concat_axis=0, tiled=True)  2.98 us
    pallas_call x1, Pallas kernels, pack(): pl.pallas_call(functools.partial(pack_kernel, cols), out_shape=jax.ShapeD...  1.44 us
  transfers between devices with their start and end apart: 2, of which 1 were waited for; matrix products, arithmetic and copies ran while one was open for 0% of the time, Pallas kernels for 29%

profile of v6, /device:TPU:0, one launch (start us, length us, event | category | flops | bytes accessed | tf_op | source)
XLA Modules:
  0.0 34.8 jit_solution(7800789957275957658)
XLA Ops:
  0.0 1.4 %pack_inputs.1 = bf16[16,16,128]{2,1,0:T(8,128)(2,1)} custom-call(s32[1,1,2,2]{3,2,1,0:T(2,128)} %tiles_ref.1, f32[3,2,128]{2,1,0:T(2,128)} %noise_ref.3, s32[3,128]{1,0:T(4,128)} %offsets_ref.1, s32[1,1,16,16]{3,2,1,0:T(8,128)} %cells_ref.1, s32[1,128]{1,0:T(1,128)} %bitcast.1), custom_call_target="tpu_custom_call" | custom-call | tf_op jit(solution)/shard_map/pack_inputs/pallas_call | solution.py:180
  1.4 7.4 %all-to-all-start = ((bf16[16,16,128]{2,1,0:T(8,128)(2,1)}), bf16[16,16,128]{2,1,0:T(8,128)(2,1)S(1)}, u32[]{:S(2)}, u32[]{:S(2)}) async-start(bf16[16,16,128]{2,1,0:T(8,128)(2,1)} %pack_inputs.1), calls=%async_computation | async-start | bytes 131072 | tf_op jit(solution)/shard_map/all_to_all | solution.py:619
  8.8 3.7 %spectrum.1 = (bf16[768,2048]{1,0:T(8,128)(2,1)S(1)}, bf16[2,128,128]{2,1,0:T(8,128)(2,1)S(1)}) custom-call(f32[2,3,2,32,32,128]{5,4,3,2,1,0:T(8,128)} %spec_hbm.1, bf16[256,256]{1,0:T(8,128)(2,1)} %constant.12.clone.turn_hbm, f32[2,128,128]{2,1,0:T(8,128)} %constant.13.clone.wave_hbm), custom_call_target="tpu_custom_call" | custom-call | flops 805306368 | bytes 9437184 | tf_op jit(solution)/shard_map/spectrum/pallas_call | solution.py:276
  12.5 3.0 %all-to-all-done.packed_ref = bf16[16,16,128]{2,1,0:T(8,128)(2,1)S(1)} async-done(((bf16[16,16,128]{2,1,0:T(8,128)(2,1)}), bf16[16,16,128]{2,1,0:T(8,128)(2,1)S(1)}, u32[]{:S(2)}, u32[]{:S(2)}) %all-to-all-start) | async-done | bytes 65568 | tf_op jit(solution)/shard_map/all_to_all | solution.py:619
  15.5 0.0 copy-start
  15.5 8.5 %sample_far.1 = f32[16,3,2,128]{3,2,1,0:T(2,128)} custom-call(bf16[16,16,128]{2,1,0:T(8,128)(2,1)S(1)} %all-to-all-done.packed_ref, bf16[768,2048]{1,0:T(8,128)(2,1)S(1)} %get-tuple-element.7.field_ref, bf16[2,128,128]{2,1,0:T(8,128)(2,1)S(1)} %get-tuple-element.8.table_ref), custom_call_target="tpu_custom_call" | custom-call | flops 6442450944 | bytes 3145728 | tf_op jit(solution)/shard_map/sample_far/pallas_call | solution.py:410
  24.0 3.7 %all-to-all-start.1 = ((f32[16,3,2,128]{3,2,1,0:T(2,128)}), f32[16,3,2,128]{3,2,1,0:T(2,128)S(1)}, u32[]{:S(2)}, u32[]{:S(2)}) async-start(f32[16,3,2,128]{3,2,1,0:T(2,128)} %sample_far.1), calls=%async_computation.1 | async-start | bytes 98304 | tf_op jit(solution)/shard_map/all_to_all | solution.py:619
  27.7 0.0 copy-done
  27.7 6.5 %near_field.1 = f32[3,2,128]{2,1,0:T(2,128)S(1)} custom-call(bf16[16,16,128]{2,1,0:T(8,128)(2,1)S(1)} %all-to-all-done.packed_ref, f32[3,2,128]{2,1,0:T(2,128)S(1)} %copy-done, bf16[2,3,2,64,896]{4,3,2,1,0:T(8,128)(2,1)} %constant.14.clone.table_hbm, bf16[3,2,256,512]{3,2,1,0:T(8,128)(2,1)} %constant.15.clone.energy_hbm, ...), custom_call_target="tpu_custom_call" | custom-call | flops 4831838208 | bytes 8000000 | tf_op jit(solution)/shard_map/near_field/pallas_call | solution.py:598
  34.2 0.0 all-to-all-done.1
  34.2 0.6 %add.3 = f32[3,2,128]{2,1,0:T(2,128)} add(f32[3,2,128]{2,1,0:T(2,128)S(1)} %near_field.1, f32[3,2,128]{2,1,0:T(2,128)S(1)} %reduce_sum.9) | non-fusion elementwise | flops 768 | bytes 9216 | tf_op jit(solution)/shard_map/add | solution.py:628
  (1 shorter events, 0.0 us)
Async XLA Ops:
  1.4 14.0 %all-to-all-start = ((bf16[16,16,128]{2,1,0:T(8,128)(2,1)}), bf16[16,16,128]{2,1,0:T(8,128)(2,1)S(1)}, u32[]{:S(2)}, u32[]{:S(2)}) async-start(bf16[16,16,128]{2,1,0:T(8,128)(2,1)} %pack_inputs.1), calls=%async_computation | async-start | bytes 131072 | tf_op jit(solution)/shard_map/all_to_all | solution.py:619
  15.5 12.2 %copy-start = (f32[3,2,128]{2,1,0:T(2,128)S(1)}, f32[3,2,128]{2,1,0:T(2,128)}, u32[]{:S(2)}) copy-start(f32[3,2,128]{2,1,0:T(2,128)} %noise_ref.3) | copy-start | bytes 9220
  24.0 10.2 %all-to-all-start.1 = ((f32[16,3,2,128]{3,2,1,0:T(2,128)}), f32[16,3,2,128]{3,2,1,0:T(2,128)S(1)}, u32[]{:S(2)}, u32[]{:S(2)}) async-start(f32[16,3,2,128]{3,2,1,0:T(2,128)} %sample_far.1), calls=%async_computation.1 | async-start | bytes 98304 | tf_op jit(solution)/shard_map/all_to_all | solution.py:619
